TPU v7x, 32 devices: a whole 2x2x4 slice. The times are simulated.
32 devices in a mesh: gx: 8 (over z, core), vert: 4 (over y, x).
Axes of the slice: x: 2, y: 2, z: 4, core: 2. Of those that a mesh axis runs over, the one named last changes fastest.
Arguments:
- distribution: float32 [4096, 8, 256], P('vert', 'gx'), may hold values from -6 to 6
- relax_rate: float32 [8, 256], P('gx'), may hold values from 0.3 to 3
- node_weight: float32 [4096], P('vert'), may hold values from 0.05 to 1
- kernel_tiles: bfloat16 [32, 128, 1536], P('vert'), may hold values from -0.15625 to 0.15625
- tile_cols: int32 [32, 12], P('vert'), may hold values from 0 to 31, as said below
Outputs:
- new_distribution: float32 [4096, 8, 256], P('vert', 'gx')
Inputs may be any that keep to these rules, and one draw needn't show every extreme that they name: `tile_cols`: row block r lists its own block r first; the 12 column blocks listed for one row block are distinct.
All inputs are finite; a program needn't handle non-finite values.
Results may differ from a plain program's by a relative error of at most 0.0021.
Values may be sent and summed in bfloat16 or wider, within the bound.
A program may use at most 64 MiB of HBM per device.

v0:
```python
import jax
import jax.numpy as jnp
from jax import lax
from jax.sharding import PartitionSpec as P

Q = 16
TILE = 128
NZ = 4
STEPS = 2
V = 4096
RBLK = 32


COURANT_SCALE = 0.3
KERNEL_STEP = 0.5
PRECISE = lax.Precision.HIGHEST


def extended(block, sides, width):
    for axis, dim in sides:
        count = lax.axis_size(axis)
        forward = [(i, i + 1) for i in range(count - 1)]
        forward.append((count - 1, 0))
        backward = [(target, source) for source, target in forward]
        low = lax.ppermute(
            lax.slice_in_dim(block, block.shape[dim] - width, None, axis=dim), axis, forward
        )
        high = lax.ppermute(lax.slice_in_dim(block, 0, width, axis=dim), axis, backward)
        block = jnp.concatenate([low, block, high], axis=dim)
    return block


def node_components(first_node, node_count):
    node_index = first_node + jnp.arange(node_count, dtype=jnp.int32)
    middle = (Q - 1) / 2.0
    speed_x = ((node_index % Q).astype(jnp.float32) - middle) / middle
    speed_y = ((node_index // Q % Q).astype(jnp.float32) - middle) / middle
    speed_z = ((node_index // (Q * Q)).astype(jnp.float32) - middle) / middle
    courant = COURANT_SCALE * jnp.stack([speed_x, speed_y, speed_z])
    squares = speed_x * speed_x + speed_y * speed_y + speed_z * speed_z
    invariants = jnp.stack([jnp.ones_like(speed_x), speed_x, speed_y, speed_z, squares])
    return (courant, invariants)


def gram_inverse(weighted, invariants):
    gram_matrix = jnp.dot(weighted, invariants.T, precision=PRECISE)
    factor = jnp.linalg.cholesky(gram_matrix)
    return jax.scipy.linalg.cho_solve((factor, True), jnp.eye(5, dtype=gram_matrix.dtype))


def advect(source, lower_x, upper_x, courant):
    plane_size = source.shape[-1]
    z_index = jnp.arange(plane_size, dtype=jnp.int32) % NZ
    lower_y = jnp.roll(source, NZ, axis=-1)
    upper_y = jnp.roll(source, -NZ, axis=-1)
    lower_z = jnp.where(
        z_index == 0, jnp.roll(source, 1 - NZ, axis=-1), jnp.roll(source, 1, axis=-1)
    )
    upper_z = jnp.where(
        z_index == NZ - 1, jnp.roll(source, NZ - 1, axis=-1), jnp.roll(source, -1, axis=-1)
    )
    total_flux = jnp.zeros_like(source)
    for component, below, above in (
        (0, lower_x, upper_x),
        (1, lower_y, upper_y),
        (2, lower_z, upper_z),
    ):
        node_speed = courant[component][:, None, None]
        total_flux = (
            total_flux
            + jnp.maximum(node_speed, 0.0) * (source - below)
            + jnp.minimum(node_speed, 0.0) * (above - source)
        )
    return source - total_flux


def apply_kernel(blocks, tile_rows, column_lists):
    cell_count = blocks.shape[-1]

    def one_block(tile_pair):
        tile_row, column_list = tile_pair
        picked = jnp.take(blocks, column_list, axis=0).reshape(-1, cell_count)
        return jnp.dot(tile_row, picked, preferred_element_type=jnp.float32)

    return lax.map(one_block, (tile_rows, column_lists))


def per_device(distribution, relax_rate, node_weight, kernel_tiles, tile_cols):
    node_local, slab_depth, plane_cells = distribution.shape
    cell_count = slab_depth * plane_cells
    first_node = lax.axis_index("vert") * node_local
    courant, invariants = node_components(first_node, node_local)
    all_weights = lax.all_gather(node_weight, "vert", axis=0, tiled=True)
    all_speeds, all_invariants = node_components(0, V)
    all_weighted = all_invariants * all_weights[None, :]
    inverse = gram_inverse(all_weighted, all_invariants)
    relax_share = relax_rate / (1.0 + relax_rate)
    current = distribution
    for step_index in range(STEPS):
        rounded = current.astype(jnp.bfloat16)
        padded = extended(current, (("gx", 1),), 1)
        lower_x = padded[:, :-2]
        upper_x = padded[:, 2:]
        advected = advect(current, lower_x, upper_x, courant)
        gathered = lax.all_gather(
            rounded.reshape(node_local, cell_count), "vert", axis=0, tiled=True
        )
        kernel_term = apply_kernel(
            gathered.reshape(RBLK, TILE, cell_count), kernel_tiles, tile_cols
        )
        explicit = advected + KERNEL_STEP * kernel_term.reshape(current.shape)
        local_weighted = invariants * node_weight[None, :]
        partial_moments = jnp.dot(
            local_weighted, explicit.reshape(node_local, cell_count), precision=PRECISE
        )
        moments = lax.psum(partial_moments, "vert")
        coeffs = jnp.dot(inverse, moments, precision=PRECISE)
        equilibrium = jnp.dot(invariants.T, coeffs, precision=PRECISE).reshape(current.shape)
        current = explicit - relax_share[None] * (explicit - equilibrium)
    return current


def solution(mesh):
    placed = (
        P("vert", "gx", None),
        P("gx", None),
        P("vert"),
        P("vert", None, None),
        P("vert", None),
    )
    return jax.shard_map(
        per_device, mesh=mesh, in_specs=placed, out_specs=P("vert", "gx", None), check_vma=False
    )
```

profile of v0, /device:TPU:0, one launch (start us, length us, event | category | flops | bytes accessed | tf_op | source)
XLA Modules:
  0.0 208.4 jit_solution(16046134361375844996)
XLA Ops:
  6.5 2.4 %copy.54 = f32[1024,1,256]{0,2,1:T(8,128)S(1)} copy(f32[1024,1,256]{2,1,0:T(1,128)} %param.11) | data formatting | bytes 2097152 | tf_op args[0]
  8.9 4.5 %collective-permute-start.1 = (f32[1024,1,256]{0,2,1:T(8,128)S(1)}, f32[1024,1,256]{0,2,1:T(8,128)}, u32[]{:S(2)}, u32[]{:S(2)}) collective-permute-start(f32[1024,1,256]{0,2,1:T(8,128)S(1)} %copy.54), channel_id=1, source_target_pairs={{4,0},{8,4},{12,8},{16,12},{20,16},{24,20},{28,24},{0,28},{5,1},{9... | collective-permute-start | bytes 3145736 | tf_op jit(solution)/shard_map/ppermute | solution.py:28
  13.5 2.1 copy.68
  15.8 8.2 %all_gather.10 = f32[4096]{0:T(1024)S(1)} all-gather(f32[1024]{0:T(1024)S(1)} %copy-done), channel_id=1, replica_groups=mesh['gx'=8,'vert'=4] {'vert'}, dimensions={0}, use_global_device_ids=true | all-gather | bytes 20480 | tf_op jit(solution)/shard_map/all_gather | solution.py:93
  32.2 20.1 %all-gather.5.cloned.1.call-done = bf16[4096,1,256]{2,0,1:T(8,128)(2,1)} async-done(((bf16[1024,1,256]{2,0,1:T(8,128)(2,1)}), bf16[4096,1,256]{2,0,1:T(8,128)(2,1)}) %all-gather.5.cloned.1.call-update) | async-done | bytes 2097168 | tf_op jit(solution)/shard_map/all_gather | solution.py:105
  52.4 34.8 %while.20 = (s32[]{:T(128)}, f32[8,128,256]{2,1,0:T(8,128)S(1)}, bf16[8,128,1536]{2,1,0:T(8,128)(2,1)}, s32[8,12]{1,0:T(8,128)}, bf16[32,128,256]{2,1,0:T(8,128)(2,1)}, /*index=5*/s32[]{:T(128)}) while((s32[]{:T(128)}, f32[8,128,256]{2,1,0:T(8,128)S(1)}, bf16[8,128,1536]{2,1,0:T(8,128)(2,1)}, s32[8,12]{1,0:T(8,128)}, ...), condition=%wide.region_1.3_spmd, body=%wide.region_0.2_spmd.sunk | while | flops 101057608 | bytes 4461865 | solution.py:85
  53.1 2.2 %gather_fusion = bf16[12,128,256]{2,1,0:T(8,128)(2,1)S(1)} fusion(bf16[32,128,256]{2,1,0:T(8,128)(2,1)} %get-tuple-element.224, s32[1024]{0:T(1024)S(1)} %pad_clamp_fusion.4), kind=kCustom, calls=%fused_computation.clone.clone.1 | custom fusion | bytes 1572912 | tf_op jit(solution)/shard_map/while/body/eval_jaxpr/jit(_take)/gather | solution.py:82
  57.4 2.2 %gather_fusion = bf16[12,128,256]{2,1,0:T(8,128)(2,1)S(1)} fusion(bf16[32,128,256]{2,1,0:T(8,128)(2,1)} %get-tuple-element.224, s32[1024]{0:T(1024)S(1)} %pad_clamp_fusion.4), kind=kCustom, calls=%fused_computation.clone.clone.1 | custom fusion | bytes 1572912 | tf_op jit(solution)/shard_map/while/body/eval_jaxpr/jit(_take)/gather | solution.py:82
  61.8 2.2 %gather_fusion = bf16[12,128,256]{2,1,0:T(8,128)(2,1)S(1)} fusion(bf16[32,128,256]{2,1,0:T(8,128)(2,1)} %get-tuple-element.224, s32[1024]{0:T(1024)S(1)} %pad_clamp_fusion.4), kind=kCustom, calls=%fused_computation.clone.clone.1 | custom fusion | bytes 1572912 | tf_op jit(solution)/shard_map/while/body/eval_jaxpr/jit(_take)/gather | solution.py:82
  66.1 2.2 %gather_fusion = bf16[12,128,256]{2,1,0:T(8,128)(2,1)S(1)} fusion(bf16[32,128,256]{2,1,0:T(8,128)(2,1)} %get-tuple-element.224, s32[1024]{0:T(1024)S(1)} %pad_clamp_fusion.4), kind=kCustom, calls=%fused_computation.clone.clone.1 | custom fusion | bytes 1572912 | tf_op jit(solution)/shard_map/while/body/eval_jaxpr/jit(_take)/gather | solution.py:82
  70.5 2.2 %gather_fusion = bf16[12,128,256]{2,1,0:T(8,128)(2,1)S(1)} fusion(bf16[32,128,256]{2,1,0:T(8,128)(2,1)} %get-tuple-element.224, s32[1024]{0:T(1024)S(1)} %pad_clamp_fusion.4), kind=kCustom, calls=%fused_computation.clone.clone.1 | custom fusion | bytes 1572912 | tf_op jit(solution)/shard_map/while/body/eval_jaxpr/jit(_take)/gather | solution.py:82
  74.8 2.2 %gather_fusion = bf16[12,128,256]{2,1,0:T(8,128)(2,1)S(1)} fusion(bf16[32,128,256]{2,1,0:T(8,128)(2,1)} %get-tuple-element.224, s32[1024]{0:T(1024)S(1)} %pad_clamp_fusion.4), kind=kCustom, calls=%fused_computation.clone.clone.1 | custom fusion | bytes 1572912 | tf_op jit(solution)/shard_map/while/body/eval_jaxpr/jit(_take)/gather | solution.py:82
  79.2 2.2 %gather_fusion = bf16[12,128,256]{2,1,0:T(8,128)(2,1)S(1)} fusion(bf16[32,128,256]{2,1,0:T(8,128)(2,1)} %get-tuple-element.224, s32[1024]{0:T(1024)S(1)} %pad_clamp_fusion.4), kind=kCustom, calls=%fused_computation.clone.clone.1 | custom fusion | bytes 1572912 | tf_op jit(solution)/shard_map/while/body/eval_jaxpr/jit(_take)/gather | solution.py:82
  83.5 2.2 %gather_fusion = bf16[12,128,256]{2,1,0:T(8,128)(2,1)S(1)} fusion(bf16[32,128,256]{2,1,0:T(8,128)(2,1)} %get-tuple-element.224, s32[1024]{0:T(1024)S(1)} %pad_clamp_fusion.4), kind=kCustom, calls=%fused_computation.clone.clone.1 | custom fusion | bytes 1572912 | tf_op jit(solution)/shard_map/while/body/eval_jaxpr/jit(_take)/gather | solution.py:82
  89.8 4.8 %fusion.22 = f32[1024,1,256]{0,2,1:T(8,128)S(1)} fusion(f32[1024,1,256]{0,2,1:T(8,128)S(1)} %copy.64, f32[1024,1,256]{0,2,1:T(8,128)S(1)} %copy.54, f32[1024,1,252]{0,2,1:T(8,128)} %get-tuple-element.117, f32[1024,1,4]{0,2,1:T(4,128)S(1)} %get-tuple-element.119, f32[1024,1,4]{0,2,1:T(4,128)S(1)} %get-tuple-element.118, ...), kind=kLoop, calls=%fused_computation.39 | loop fusion | flops 7077888 | bytes 11559424 | tf_op jit(solution)/shard_map/add | solution.py:111
  95.5 9.1 %psum.14 = f32[5,256]{1,0:T(8,128)S(1)} all-reduce(f32[5,256]{1,0:T(8,128)S(1)} %fusion.42), channel_id=1, replica_groups=mesh['gx'=8,'vert'=4] {'vert'}, use_global_device_ids=true, to_apply=%region_4.6 | all-reduce | flops 1280 | bytes 10240 | tf_op jit(solution)/shard_map/psum | solution.py:116
  104.7 1.9 fusion.88
  110.6 1.6 fusion.76
  112.2 29.9 %all-gather.7.cloned.1.call-done = bf16[4096,1,256]{0,2,1:T(8,128)(2,1)} async-done(((bf16[1024,1,256]{0,2,1:T(8,128)(2,1)}), bf16[4096,1,256]{0,2,1:T(8,128)(2,1)}) %all-gather.7.cloned.1.call-update) | async-done | bytes 2097168 | tf_op jit(solution)/shard_map/all_gather | solution.py:105
  142.1 4.1 %copy.65 = bf16[4096,1,256]{2,0,1:T(8,128)(2,1)} copy(bf16[4096,1,256]{0,2,1:T(8,128)(2,1)} %all-gather.7.cloned.1.call-done) | data formatting | bytes 4194304 | tf_op jit(solution)/shard_map/while | solution.py:85
  146.2 34.8 %while.21 = (s32[]{:T(128)}, f32[8,128,256]{2,1,0:T(8,128)S(1)}, bf16[8,128,1536]{2,1,0:T(8,128)(2,1)}, s32[8,12]{1,0:T(8,128)}, bf16[32,128,256]{2,1,0:T(8,128)(2,1)}, /*index=5*/s32[]{:T(128)}) while((s32[]{:T(128)}, f32[8,128,256]{2,1,0:T(8,128)S(1)}, bf16[8,128,1536]{2,1,0:T(8,128)(2,1)}, s32[8,12]{1,0:T(8,128)}, ...), condition=%wide.region_6.8_spmd, body=%wide.region_5.7_spmd.sunk | while | flops 101057608 | bytes 4461865 | solution.py:85
  147.0 2.2 %gather_fusion.1 = bf16[12,128,256]{2,1,0:T(8,128)(2,1)S(1)} fusion(bf16[32,128,256]{2,1,0:T(8,128)(2,1)} %get-tuple-element.242, s32[1024]{0:T(1024)S(1)} %pad_clamp_fusion.5), kind=kCustom, calls=%fused_computation.1.clone.clone.1 | custom fusion | bytes 1572912 | tf_op jit(solution)/shard_map/while/body/eval_jaxpr/jit(_take)/gather | solution.py:82
  151.3 2.2 %gather_fusion.1 = bf16[12,128,256]{2,1,0:T(8,128)(2,1)S(1)} fusion(bf16[32,128,256]{2,1,0:T(8,128)(2,1)} %get-tuple-element.242, s32[1024]{0:T(1024)S(1)} %pad_clamp_fusion.5), kind=kCustom, calls=%fused_computation.1.clone.clone.1 | custom fusion | bytes 1572912 | tf_op jit(solution)/shard_map/while/body/eval_jaxpr/jit(_take)/gather | solution.py:82
  155.7 2.2 %gather_fusion.1 = bf16[12,128,256]{2,1,0:T(8,128)(2,1)S(1)} fusion(bf16[32,128,256]{2,1,0:T(8,128)(2,1)} %get-tuple-element.242, s32[1024]{0:T(1024)S(1)} %pad_clamp_fusion.5), kind=kCustom, calls=%fused_computation.1.clone.clone.1 | custom fusion | bytes 1572912 | tf_op jit(solution)/shard_map/while/body/eval_jaxpr/jit(_take)/gather | solution.py:82
  160.0 2.2 %gather_fusion.1 = bf16[12,128,256]{2,1,0:T(8,128)(2,1)S(1)} fusion(bf16[32,128,256]{2,1,0:T(8,128)(2,1)} %get-tuple-element.242, s32[1024]{0:T(1024)S(1)} %pad_clamp_fusion.5), kind=kCustom, calls=%fused_computation.1.clone.clone.1 | custom fusion | bytes 1572912 | tf_op jit(solution)/shard_map/while/body/eval_jaxpr/jit(_take)/gather | solution.py:82
  164.3 2.2 %gather_fusion.1 = bf16[12,128,256]{2,1,0:T(8,128)(2,1)S(1)} fusion(bf16[32,128,256]{2,1,0:T(8,128)(2,1)} %get-tuple-element.242, s32[1024]{0:T(1024)S(1)} %pad_clamp_fusion.5), kind=kCustom, calls=%fused_computation.1.clone.clone.1 | custom fusion | bytes 1572912 | tf_op jit(solution)/shard_map/while/body/eval_jaxpr/jit(_take)/gather | solution.py:82
  168.7 2.2 %gather_fusion.1 = bf16[12,128,256]{2,1,0:T(8,128)(2,1)S(1)} fusion(bf16[32,128,256]{2,1,0:T(8,128)(2,1)} %get-tuple-element.242, s32[1024]{0:T(1024)S(1)} %pad_clamp_fusion.5), kind=kCustom, calls=%fused_computation.1.clone.clone.1 | custom fusion | bytes 1572912 | tf_op jit(solution)/shard_map/while/body/eval_jaxpr/jit(_take)/gather | solution.py:82
  173.0 2.2 %gather_fusion.1 = bf16[12,128,256]{2,1,0:T(8,128)(2,1)S(1)} fusion(bf16[32,128,256]{2,1,0:T(8,128)(2,1)} %get-tuple-element.242, s32[1024]{0:T(1024)S(1)} %pad_clamp_fusion.5), kind=kCustom, calls=%fused_computation.1.clone.clone.1 | custom fusion | bytes 1572912 | tf_op jit(solution)/shard_map/while/body/eval_jaxpr/jit(_take)/gather | solution.py:82
  177.4 2.2 %gather_fusion.1 = bf16[12,128,256]{2,1,0:T(8,128)(2,1)S(1)} fusion(bf16[32,128,256]{2,1,0:T(8,128)(2,1)} %get-tuple-element.242, s32[1024]{0:T(1024)S(1)} %pad_clamp_fusion.5), kind=kCustom, calls=%fused_computation.1.clone.clone.1 | custom fusion | bytes 1572912 | tf_op jit(solution)/shard_map/while/body/eval_jaxpr/jit(_take)/gather | solution.py:82
  183.7 4.7 %fusion.34 = f32[1024,1,256]{0,2,1:T(8,128)S(1)} fusion(f32[1024,1,256]{0,2,1:T(8,128)S(1)} %copy.66, f32[1024,1,256]{0,2,1:T(8,128)S(1)} %get-tuple-element.127, f32[1024,1,252]{0,2,1:T(8,128)} %get-tuple-element.105, f32[1024,1,4]{0,2,1:T(4,128)S(1)} %get-tuple-element.107, f32[1024,1,4]{0,2,1:T(4,128)S(1)} %get-tuple-element.106, ...), kind=kLoop, calls=%fused_computation.55 | loop fusion | flops 7077888 | bytes 11559424 | tf_op jit(solution)/shard_map/add | solution.py:111
  189.3 9.1 %psum.15 = f32[5,256]{1,0:T(8,128)S(1)} all-reduce(f32[5,256]{1,0:T(8,128)S(1)} %fusion.40), channel_id=1, replica_groups=mesh['gx'=8,'vert'=4] {'vert'}, use_global_device_ids=true, to_apply=%region_7.9 | all-reduce | flops 1280 | bytes 10240 | tf_op jit(solution)/shard_map/psum | solution.py:116
  199.6 1.9 copy.62
  (123 shorter events, 54.7 us)
Async XLA Ops:
  6.5 9.2 %copy-start = (f32[1024]{0:T(1024)S(1)}, f32[1024]{0:T(1024)}, u32[]{:S(2)}) copy-start(f32[1024]{0:T(1024)} %param.13) | copy-start | bytes 12292
  6.5 20.5 %copy-start.1 = (f32[1,256]{1,0:T(1,128)S(1)}, f32[1,256]{1,0:T(1,128)}, u32[]{:S(2)}) copy-start(f32[1,256]{1,0:T(1,128)} %param.12) | copy-start | bytes 3076
  6.5 45.7 %all-gather.5.cloned.1.call-start = ((), (), s32[]{:S(2)}) async-start(), calls=%async_computation | async-start | bytes 2621440 | tf_op jit(solution)/shard_map/all_gather | solution.py:105
  8.9 80.9 %collective-permute-start.1 = (f32[1024,1,256]{0,2,1:T(8,128)S(1)}, f32[1024,1,256]{0,2,1:T(8,128)}, u32[]{:S(2)}, u32[]{:S(2)}) collective-permute-start(f32[1024,1,256]{0,2,1:T(8,128)S(1)} %copy.54), channel_id=1, source_target_pairs={{4,0},{8,4},{12,8},{16,12},{20,16},{24,20},{28,24},{0,28},{5,1},{9... | collective-permute-start | bytes 3145736 | tf_op jit(solution)/shard_map/ppermute | solution.py:28
  13.5 76.3 %collective-permute-start = (f32[1024,1,256]{0,2,1:T(8,128)S(1)}, f32[1024,1,256]{0,2,1:T(8,128)}, u32[]{:S(2)}, u32[]{:S(2)}) collective-permute-start(f32[1024,1,256]{0,2,1:T(8,128)S(1)} %copy.54), channel_id=1, source_target_pairs={{0,4},{4,8},{8,12},{12,16},{16,20},{20,24},{24,28},{28,0},{1,5},{5... | collective-permute-start | bytes 3145736 | tf_op jit(solution)/shard_map/ppermute | solution.py:25
  15.6 126.5 %all-gather.7.cloned.1.call-start = ((), (), s32[]{:S(2)}) async-start(), calls=%async_computation.1 | async-start | bytes 2621440 | tf_op jit(solution)/shard_map/all_gather | solution.py:105
  106.6 77.0 %collective-permute-start.3 = (f32[1024,1,256]{0,2,1:T(8,128)S(1)}, f32[1024,1,256]{0,2,1:T(8,128)}, u32[]{:S(2)}, u32[]{:S(2)}) collective-permute-start(f32[1024,1,256]{0,2,1:T(8,128)S(1)} %get-tuple-element.127), channel_id=1, source_target_pairs={{4,0},{8,4},{12,8},{16,12},{20,16},{24,20},{28,24},{0,28},{5,1},{9... | collective-permute-start | bytes 3145736 | tf_op jit(solution)/shard_map/ppermute | solution.py:28
  107.4 76.2 %collective-permute-start.2 = (f32[1024,1,256]{0,2,1:T(8,128)S(1)}, f32[1024,1,256]{0,2,1:T(8,128)}, u32[]{:S(2)}, u32[]{:S(2)}) collective-permute-start(f32[1024,1,256]{0,2,1:T(8,128)S(1)} %get-tuple-element.127), channel_id=1, source_target_pairs={{0,4},{4,8},{8,12},{12,16},{16,20},{20,24},{24,28},{28,0},{1,5},{5... | collective-permute-start | bytes 3145736 | tf_op jit(solution)/shard_map/ppermute | solution.py:25
Sparse Core Ops, SparseCore 0:
  15.7 36.5 all-gather.4
  106.8 35.2 all-gather.6
where the time goes:
time: 210 us; the launch traced here: 208 us
  local copies, waits for them, and re-layouts  58.5 us (28%)
  waiting for transfers between devices  50 us (24%)
  other arithmetic  27.7 us (13%)
  blocking collectives  26.3 us (13%)
  matrix products  26.1 us (12%)
  between operations  13.7 us (7%)
  starting transfers between devices  5.39 us (3%)
    all_gather x2, waiting for transfers between devices, per_device(): lax.all_gather(rounded.reshape(node_local, cell_count), 'vert', axis=0, t...  50 us
    gather x16, local copies, waits for them, and re-layouts, one_block(): picked = jnp.take(blocks, column_list, axis=0).reshape(-1, cell_count)  35 us
    dot_general x16, matrix products, one_block(): return jnp.dot(tile_row, picked, preferred_element_type=jnp.float32)  20.4 us
    psum x2, blocking collectives, per_device(): moments = lax.psum(partial_moments, 'vert')  18.2 us
    and x16, other arithmetic, one_block(): picked = jnp.take(blocks, column_list, axis=0).reshape(-1, cell_count)  11.2 us
    add x2, other arithmetic, per_device(): explicit = advected + KERNEL_STEP * kernel_term.reshape(current.shape)  9.5 us
    all_gather x1, blocking collectives, per_device(): all_weights = lax.all_gather(node_weight, 'vert', axis=0, tiled=True)  8.17 us
    ppermute x2, starting transfers between devices, extended(): lax.ppermute(lax.slice_in_dim(block, 0, width, axis=dim), axis, backward)  5.34 us
  transfers between devices with their start and end apart: 6, of which 2 were waited for; matrix products, arithmetic and copies ran while one was open for 45% of the time, Pallas kernels for 0%

commit v1 on v0

v1 whole, which is shorter than its diff:
```python
import functools

import jax
import jax.numpy as jnp
from jax import lax
from jax.experimental import pallas as pl
from jax.experimental.pallas import tpu as pltpu
from jax.sharding import PartitionSpec as P

Q = 16
TILE = 128
NZ = 4
STEPS = 2
V = 4096
RBLK = 32
CHUNK = 256
PART = 128
COURANT_SCALE = 0.3
KERNEL_STEP = 0.5
MESH = pl.DeviceIdType.MESH
F32 = jnp.float32
BF16 = jnp.bfloat16


def speeds(node_index):
    middle = (Q - 1) / 2.0
    speed_x = ((node_index & (Q - 1)).astype(F32) - middle) / middle
    speed_y = ((lax.shift_right_logical(node_index, 4) & (Q - 1)).astype(F32) - middle) / middle
    speed_z = (lax.shift_right_logical(node_index, 8).astype(F32) - middle) / middle
    return speed_x, speed_y, speed_z


def row_speeds(first, rows):
    return speeds(first + lax.broadcasted_iota(jnp.int32, (rows, 1), 0))


def vert_plan(me, count, chunks):
    if count == 4:
        x, y = lax.rem(me, 2), lax.div(me, 2)
        px, py, pd = y * 2 + (1 - x), (1 - y) * 2 + x, 3 - me
        half = chunks // 2
        first = list(range(half))
        second = list(range(half, chunks))
        to_x = [(c, px, me, c) for c in first + second]
        to_y = [(chunks + c, py, me, c) for c in second + first]
        own = [send for pair in zip(to_x, to_y) for send in pair]
        from_x = [(c, px, c) for c in first + second]
        from_y = [(chunks + c, py, c) for c in second + first]
        arrivals = [item for pair in zip(from_x, from_y) for item in pair]
        forwards = {}
        for c in first:
            forwards[c] = (2 * chunks + c, py, px, c)
        for c in second:
            forwards[chunks + c] = (2 * chunks + c, px, py, c)
        late = [c for pair in zip(first, second) for c in pair]
        arrivals += [(2 * chunks + c, pd, c) for c in late]
        return own, arrivals, forwards
    own, arrivals = [], []
    for p in range(1, count):
        for c in range(chunks):
            key = (p - 1) * chunks + c
            own.append((key, lax.rem(me + p, count), me, c))
            arrivals.append((key, lax.rem(me + count - p, count), c))
    return own, arrivals, {}


def kernel(
    count, slabs, place_ref, tiles_ref, dist_ref, relax_ref, weight_ref, out_ref,
    tiles, dense, state, acc, gathered, plane_out, plane_in, mom_out, mom_in, gram_out, gram_in,
    weights2, tile_sem, vert_send, vert_recv, plane_send, plane_recv, mom_send, mom_recv,
    gram_send, gram_recv,
):
    rows, cells = state.shape
    chunks = rows // CHUNK
    row_blocks = rows // TILE
    listed = tiles_ref.shape[2] // TILE
    me = lax.axis_index("vert")
    slab = lax.axis_index("gx")
    above = lax.rem(slab + 1, slabs)
    below = lax.rem(slab + slabs - 1, slabs)
    first_node = me * rows

    loads = [
        pltpu.make_async_copy(
            tiles_ref.at[:, :, pl.ds(j * TILE, TILE)], tiles.at[j], tile_sem.at[j]
        )
        for j in range(listed)
    ]
    for load in loads:
        load.start()

    barrier = pltpu.get_barrier_semaphore()
    for p in range(1, count):
        pl.semaphore_signal(
            barrier, inc=1, device_id=(slab, lax.rem(me + p, count)), device_id_type=MESH
        )
    for other in (below, above):
        pl.semaphore_signal(barrier, inc=1, device_id=(other, me), device_id_type=MESH)
    pl.semaphore_wait(barrier, count + 1)

    own, arrivals, forwards = vert_plan(me, count, chunks)
    pending = []

    def vert_copy(step, key, target, block, chunk):
        where = gathered.at[step, block * chunks + chunk]
        return pltpu.make_async_remote_copy(
            src_ref=where, dst_ref=where, send_sem=vert_send.at[step, key],
            recv_sem=vert_recv.at[step, key], device_id=(slab, target), device_id_type=MESH,
        )

    def plane_copy(step, side):
        return pltpu.make_async_remote_copy(
            src_ref=plane_out.at[step, side], dst_ref=plane_in.at[step, side],
            send_sem=plane_send.at[step, side], recv_sem=plane_recv.at[step, side],
            device_id=(above if side == 1 else below, me), device_id_type=MESH,
        )

    def small_copy(out, into, send, recv, p):
        return pltpu.make_async_remote_copy(
            src_ref=out, dst_ref=into, send_sem=send, recv_sem=recv,
            device_id=(slab, lax.rem(me + p, count)), device_id_type=MESH,
        )

    def publish(step, base, part):
        chunk, inner = base // CHUNK, base % CHUNK
        gathered[step, me * chunks + chunk, pl.ds(inner, PART), :] = part.astype(BF16)
        groups = part.reshape(PART // Q, 2, Q // 2, cells)
        for side in range(2):
            plane_out[step, side, pl.ds(base // 2, PART // 2), :] = (
                groups[:, side].reshape(PART // 2, cells).astype(BF16)
            )

    def send_all(step):
        for key, target, block, chunk in own:
            copy = vert_copy(step, key, target, block, chunk)
            copy.start()
            pending.append(copy)
        for side in range(2):
            copy = plane_copy(step, side)
            copy.start()
            pending.append(copy)

    for base in range(0, rows, PART):
        left = dist_ref[pl.ds(2 * base, PART, stride=2), :]
        right = dist_ref[pl.ds(2 * base + 1, PART, stride=2), :]
        part = jnp.concatenate([left, right], axis=1)
        state[pl.ds(base, PART), :] = part
        publish(0, base, part)
    send_all(0)

    lane_node = first_node + lax.broadcasted_iota(jnp.int32, (8, rows), 1)
    kind = lax.broadcasted_iota(jnp.int32, (8, rows), 0)
    sx, sy, sz = speeds(lane_node)
    kinds = [jnp.ones_like(sx), sx, sy, sz, sx * sx + sy * sy + sz * sz]
    invariants = jnp.zeros_like(sx)
    for k, row in enumerate(kinds):
        invariants = jnp.where(kind == k, row, invariants)
    weighted = invariants * weight_ref[...]
    high = weighted.astype(BF16).astype(F32)
    weights2[...] = jnp.concatenate([high, weighted - high], axis=0).astype(BF16)
    for l in range(5):
        column = jnp.sum(weighted * kinds[l], axis=1, keepdims=True)
        gram_out[l] = jnp.broadcast_to(column, (8, 128))
    for p in range(1, count):
        copy = small_copy(
            gram_out, gram_in.at[p - 1], gram_send.at[p - 1], gram_recv.at[p - 1], p
        )
        copy.start()
        pending.append(copy)

    tiles[listed] = jnp.zeros((row_blocks, TILE, TILE), BF16)
    for load in loads:
        load.wait()
    per_chunk = CHUNK // TILE

    def expand(index, carry):
        k, r = lax.div(index, row_blocks), lax.rem(index, row_blocks)
        for b in range(per_chunk):
            place = place_ref[r, k * per_chunk + b]
            dense[k, pl.ds(pl.multiple_of(r * TILE, TILE), TILE), pl.ds(b * TILE, TILE)] = tiles[
                place, r
            ]
        return carry

    lax.fori_loop(0, (V // CHUNK) * row_blocks, expand, 0, unroll=4)

    def advect(step):
        def one(i, carry):
            base = pl.multiple_of(i * PART, PART)
            source = state[pl.ds(base, PART), :]
            sides = [
                plane_in[step, side, pl.ds(pl.multiple_of(i * (PART // 2), PART // 2), PART // 2), :]
                .astype(F32)
                .reshape(PART // Q, 1, Q // 2, cells)
                for side in range(2)
            ]
            upwind_x = jnp.concatenate(sides, axis=1).reshape(PART, cells)
            px, py, pz = [COURANT_SCALE * s for s in row_speeds(first_node + base, PART)]
            z_index = lax.broadcasted_iota(jnp.int32, (PART, cells), 1) & (NZ - 1)
            lower_y = pltpu.roll(source, NZ, 1)
            upper_y = pltpu.roll(source, cells - NZ, 1)
            lower_z = jnp.where(
                z_index == 0, pltpu.roll(source, cells + 1 - NZ, 1), pltpu.roll(source, 1, 1)
            )
            upper_z = jnp.where(
                z_index == NZ - 1, pltpu.roll(source, NZ - 1, 1), pltpu.roll(source, cells - 1, 1)
            )
            flux = jnp.abs(px) * (source - upwind_x)
            flux += jnp.maximum(py, 0.0) * (source - lower_y) + jnp.minimum(py, 0.0) * (
                upper_y - source
            )
            flux += jnp.maximum(pz, 0.0) * (source - lower_z) + jnp.minimum(pz, 0.0) * (
                upper_z - source
            )
            acc[pl.ds(base, PART), :] = source - flux
            return carry

        lax.fori_loop(0, rows // PART, one, 0)

    def multiply(step, index):
        def one(i, carry):
            here = pl.ds(pl.multiple_of(i * CHUNK, CHUNK), CHUNK)
            acc[here, :] += KERNEL_STEP * jnp.dot(
                dense[index, here, :], gathered[step, index], preferred_element_type=F32
            )
            return carry

        lax.fori_loop(0, rows // CHUNK, one, 0, unroll=True)

    share = relax_ref[...] / (1.0 + relax_ref[...])
    inverse = None

    for step in range(STEPS):
        forwarded = 0

        def arrive(item, step=step):
            key, block, chunk = item
            vert_copy(step, key, me, block, chunk).wait_recv()
            if key in forwards:
                copy = vert_copy(step, *forwards[key])
                copy.start()
                pending.append(copy)
            return block * chunks + chunk

        early = [item for item in arrivals if item[0] in forwards]
        rest = [item for item in arrivals if item[0] not in forwards]
        ready = [me * chunks + c for c in range(chunks)]
        for side in range(2):
            plane_copy(step, side).wait_recv()
        advect(step)
        for index in ready[: chunks // 2]:
            multiply(step, index)
        landed = [arrive(item) for item in early]
        for index in ready[chunks // 2 :] + landed:
            multiply(step, index)
        for item in rest:
            multiply(step, arrive(item))

        total = jnp.zeros((16, cells), F32)
        for base in range(0, rows, CHUNK):
            explicit = acc[pl.ds(base, CHUNK), :]
            top = explicit.astype(BF16)
            low = (explicit - top.astype(F32)).astype(BF16)
            left = weights2[:, pl.ds(base, CHUNK)]
            total += jnp.dot(left, top, preferred_element_type=F32)
            total += jnp.dot(left, low, preferred_element_type=F32)
        mom_out[step] = total[:8] + total[8:]
        for p in range(1, count):
            copy = small_copy(
                mom_out.at[step], mom_in.at[step, p - 1], mom_send.at[step, p - 1],
                mom_recv.at[step, p - 1], p,
            )
            copy.start()
            pending.append(copy)

        if inverse is None:
            gram = gram_out[...]
            for p in range(1, count):
                small_copy(
                    gram_out, gram_in.at[p - 1], gram_send.at[p - 1], gram_recv.at[p - 1], p
                ).wait_recv()
                gram += gram_in[p - 1]
            matrix = [[gram[l, k : k + 1, :] for l in range(5)] for k in range(5)]
            one, none = jnp.ones((1, 128), F32), jnp.zeros((1, 128), F32)
            inverse = [[one if k == l else none for l in range(5)] for k in range(5)]
            for k in range(5):
                scale = 1.0 / matrix[k][k]
                matrix[k] = [entry * scale for entry in matrix[k]]
                inverse[k] = [entry * scale for entry in inverse[k]]
                for r in range(5):
                    if r != k:
                        factor = matrix[r][k]
                        matrix[r] = [a - factor * b for a, b in zip(matrix[r], matrix[k])]
                        inverse[r] = [a - factor * b for a, b in zip(inverse[r], inverse[k])]
            inverse = [
                [jnp.concatenate([entry] * (cells // 128), axis=1) for entry in line]
                for line in inverse
            ]

        moments = mom_out[step]
        for p in range(1, count):
            small_copy(
                mom_out.at[step], mom_in.at[step, p - 1], mom_send.at[step, p - 1],
                mom_recv.at[step, p - 1], p,
            ).wait_recv()
            moments += mom_in[step, p - 1]
        coeffs = [
            share * sum(inverse[k][l] * moments[l : l + 1, :] for l in range(5)) for k in range(5)
        ]
        keep = 1.0 - share
        for base in range(0, rows, PART):
            vx, vy, vz = row_speeds(first_node + base, PART)
            squares = vx * vx + vy * vy + vz * vz
            equilibrium = (
                coeffs[0] + vx * coeffs[1] + vy * coeffs[2] + vz * coeffs[3] + squares * coeffs[4]
            )
            part = keep * acc[pl.ds(base, PART), :] + equilibrium
            if step + 1 < STEPS:
                state[pl.ds(base, PART), :] = part
                publish(step + 1, base, part)
            else:
                out_ref[pl.ds(2 * base, PART, stride=2), :] = part[:, :128]
                out_ref[pl.ds(2 * base + 1, PART, stride=2), :] = part[:, 128:]
        if step + 1 < STEPS:
            send_all(step + 1)

    for copy in pending:
        copy.wait_send()


def per_device(count, slabs, distribution, relax_rate, node_weight, kernel_tiles, tile_cols):
    rows, depth, cells = distribution.shape
    assert depth == 1 and cells == 256 and rows % CHUNK == 0
    row_blocks, listed = tile_cols.shape
    chunks = rows // CHUNK
    slots = jnp.arange(listed, dtype=jnp.int32)[None, :, None]
    match = tile_cols[:, :, None] == jnp.arange(RBLK, dtype=jnp.int32)[None, None, :]
    places = listed + jnp.sum(jnp.where(match, slots - listed, 0), axis=1)
    keys = 3 * chunks if count == 4 else (count - 1) * chunks
    peers = count - 1
    vmem = pl.BlockSpec(memory_space=pltpu.VMEM)
    dma = pltpu.SemaphoreType.DMA
    result = pl.pallas_call(
        functools.partial(kernel, count, slabs),
        out_shape=jax.ShapeDtypeStruct((rows * 2, 128), F32),
        in_specs=[
            pl.BlockSpec(memory_space=pltpu.SMEM),
            pl.BlockSpec(memory_space=pl.ANY),
            vmem, vmem, vmem,
        ],
        out_specs=vmem,
        scratch_shapes=[
            pltpu.VMEM((listed + 1, row_blocks, TILE, TILE), BF16),
            pltpu.VMEM((V // CHUNK, rows, CHUNK), BF16),
            pltpu.VMEM((rows, cells), F32),
            pltpu.VMEM((rows, cells), F32),
            pltpu.VMEM((STEPS, V // CHUNK, CHUNK, cells), BF16),
            pltpu.VMEM((STEPS, 2, rows // 2, cells), BF16),
            pltpu.VMEM((STEPS, 2, rows // 2, cells), BF16),
            pltpu.VMEM((STEPS, 8, cells), F32),
            pltpu.VMEM((STEPS, peers, 8, cells), F32),
            pltpu.VMEM((5, 8, 128), F32),
            pltpu.VMEM((peers, 5, 8, 128), F32),
            pltpu.VMEM((16, rows), BF16),
            dma((listed,)),
            dma((STEPS, keys)),
            dma((STEPS, keys)),
            dma((STEPS, 2)),
            dma((STEPS, 2)),
            dma((STEPS, peers)),
            dma((STEPS, peers)),
            dma((peers,)),
            dma((peers,)),
        ],
        compiler_params=pltpu.CompilerParams(
            collective_id=0, has_side_effects=True, vmem_limit_bytes=48 * 1024 * 1024
        ),
        name="bgk_steps",
    )(
        places, kernel_tiles, distribution.reshape(rows * 2, 128), relax_rate,
        node_weight.reshape(1, rows),
    )
    return result.reshape(rows, depth, cells)


def solution(mesh):
    placed = (
        P("vert", "gx", None),
        P("gx", None),
        P("vert"),
        P("vert", None, None),
        P("vert", None),
    )
    return jax.shard_map(
        functools.partial(per_device, mesh.shape["vert"], mesh.shape["gx"]),
        mesh=mesh, in_specs=placed, out_specs=P("vert", "gx", None), check_vma=False,
    )
```

time: 210 us -> 58.5 us (0.28)
  local copies, waits for them, and re-layouts: 58.5 us -> 6.21 us
  Pallas kernels: 0 us -> 51.9 us
  waiting for transfers between devices: 50 us -> 0 us
  other arithmetic: 27.7 us -> 0.1 us
  blocking collectives: 26.3 us -> 0 us
  matrix products: 26.1 us -> 0 us
  between operations: 13.7 us -> 0.04 us
  starting transfers between devices: 5.39 us -> 0 us
    pallas_call x0 -> x1, Pallas kernels: none -> 51.9 us  [per_device(): pl.pallas_call(functools.partial(kernel, count, slabs), out_shape=jax.Sha...]
    all_gather x2 -> x0, waiting for transfers between devices: 50 us -> none  [per_device(): lax.all_gather(rounded.reshape(node_local, cell_count), 'vert', axis=0, t...]
    gather x16 -> x0, local copies, waits for them, and re-layouts: 35 us -> none  [one_block(): picked = jnp.take(blocks, column_list, axis=0).reshape(-1, cell_count)]
    dot_general x23 -> x0, matrix products: 25.8 us -> none  [the longest x16 20.4 us: one_block(): return jnp.dot(tile_row, picked, preferred_element_type=jnp.float32)]
    psum x2 -> x0, blocking collectives: 18.2 us -> none  [per_device(): moments = lax.psum(partial_moments, 'vert')]
    and x16 -> x0, other arithmetic: 11.2 us -> none  [one_block(): picked = jnp.take(blocks, column_list, axis=0).reshape(-1, cell_count)]
    add x3 -> x1, other arithmetic: 9.58 us -> 0.01 us  [per_device(): places = listed + jnp.sum(jnp.where(match, slots - listed, 0), axis=1)]
    slice x12 -> x0, local copies, waits for them, and re-layouts: 9.49 us -> none  [the longest x4 3.28 us: advect(): jnp.roll(source, -1, axis=-1)]
  transfers between devices with their start and end apart: 6 -> 0, of which waited for: 2 -> 0; matrix products, arithmetic and copies ran while one was open for 45% -> 0% of each run, Pallas kernels for 0% -> 0%
where the time goes in v1:
time: 58.5 us; the launch traced here: 58.2 us
  Pallas kernels  51.9 us (89%)
  local copies, waits for them, and re-layouts  6.21 us (11%)
    pallas_call x1, Pallas kernels, per_device(): pl.pallas_call(functools.partial(kernel, count, slabs), out_shape=jax.Sha...  51.9 us
    unnamed x10, local copies, waits for them, and re-layouts  6.21 us

profile of v1, /device:TPU:0, one launch (start us, length us, event | category | flops | bytes accessed | tf_op | source)
XLA Modules:
  0.0 58.2 jit_solution(2954102810037615506)
XLA Ops:
  0.0 0.8 %copy.7 = s32[8,12]{0,1:T(8,128)S(1)} copy(s32[8,12]{1,0:T(8,128)} %param.9) | data formatting | bytes 768 | tf_op args[4]
  0.8 0.1 select_reduce_fusion
  0.9 0.0 copy-start
  0.9 1.9 %copy-done = bf16[8,128,1536]{2,1,0:T(8,128)(2,1)S(1)} copy-done((bf16[8,128,1536]{2,1,0:T(8,128)(2,1)S(1)}, bf16[8,128,1536]{2,1,0:T(8,128)(2,1)}, u32[]{:S(2)}) %copy-start) | copy-done | bytes 3145752
  2.8 0.0 copy-start.1
  2.8 1.2 %copy-done.1 = f32[1024,1,256]{2,1,0:T(1,128)S(1)} copy-done((f32[1024,1,256]{2,1,0:T(1,128)S(1)}, f32[1024,1,256]{2,1,0:T(1,128)}, u32[]{:S(2)}) %copy-start.1) | copy-done | bytes 1048600
  4.0 0.0 copy-start.2
  4.0 0.7 %copy-done.2 = f32[1024]{0:T(1024)S(1)} copy-done((f32[1024]{0:T(1024)S(1)}, f32[1024]{0:T(1024)}, u32[]{:S(2)}) %copy-start.2) | copy-done | bytes 4120
  4.7 0.0 copy-start.3
  4.7 0.7 %copy-done.3 = f32[1,256]{1,0:T(1,128)S(1)} copy-done((f32[1,256]{1,0:T(1,128)S(1)}, f32[1,256]{1,0:T(1,128)}, u32[]{:S(2)}) %copy-start.3) | copy-done | bytes 1048
  5.4 51.9 %bgk_steps.1 = f32[2048,128]{1,0:T(8,128)S(1)} custom-call(s32[8,32]{1,0:T(8,128)S(1)} %broadcast_add_fusion.place_ref, bf16[8,128,1536]{2,1,0:T(8,128)(2,1)S(1)} %copy-done, f32[2048,128]{1,0:T(8,128)S(1)} %bitcast.4, f32[1,256]{1,0:T(1,128)S(1)} %copy-done.3, f32[1,1024]{1,0:T(1,128)S(1)} %bitcast.5), custom_call_target="tpu_custom_call" | custom-call | tf_op jit(solution)/shard_map/bgk_steps/pallas_call | solution.py:343
  57.2 1.0 %copy.10 = f32[1024,1,256]{2,1,0:T(1,128)} copy(f32[1024,1,256]{2,1,0:T(1,128)S(1)} %bitcast.3) | data formatting | bytes 2097152
  (2 shorter events, 0.0 us)
Async XLA Ops:
  0.9 1.9 %copy-start = (bf16[8,128,1536]{2,1,0:T(8,128)(2,1)S(1)}, bf16[8,128,1536]{2,1,0:T(8,128)(2,1)}, u32[]{:S(2)}) copy-start(bf16[8,128,1536]{2,1,0:T(8,128)(2,1)} %tiles_ref.1) | copy-start | bytes 9437188
  2.8 1.2 %copy-start.1 = (f32[1024,1,256]{2,1,0:T(1,128)S(1)}, f32[1024,1,256]{2,1,0:T(1,128)}, u32[]{:S(2)}) copy-start(f32[1024,1,256]{2,1,0:T(1,128)} %param.5) | copy-start | bytes 3145732
  4.0 0.7 %copy-start.2 = (f32[1024]{0:T(1024)S(1)}, f32[1024]{0:T(1024)}, u32[]{:S(2)}) copy-start(f32[1024]{0:T(1024)} %param.7) | copy-start | bytes 12292
  4.7 0.7 %copy-start.3 = (f32[1,256]{1,0:T(1,128)S(1)}, f32[1,256]{1,0:T(1,128)}, u32[]{:S(2)}) copy-start(f32[1,256]{1,0:T(1,128)} %relax_ref.1) | copy-start | bytes 3076

commit v2 on v1

v2 whole, which is shorter than its diff:
```python
import functools

import jax
import jax.numpy as jnp
from jax import lax
from jax.experimental import pallas as pl
from jax.experimental.pallas import tpu as pltpu
from jax.sharding import PartitionSpec as P

Q = 16
TILE = 128
NZ = 4
STEPS = 2
HALVES = 2
V = 4096
RBLK = 32
CHUNK = 256
PART = 128
COURANT_SCALE = 0.3
KERNEL_STEP = 0.5
MESH = pl.DeviceIdType.MESH
F32 = jnp.float32
BF16 = jnp.bfloat16


def speeds(node_index):
    middle = (Q - 1) / 2.0
    speed_x = ((node_index & (Q - 1)).astype(F32) - middle) / middle
    speed_y = ((lax.shift_right_logical(node_index, 4) & (Q - 1)).astype(F32) - middle) / middle
    speed_z = (lax.shift_right_logical(node_index, 8).astype(F32) - middle) / middle
    return speed_x, speed_y, speed_z


def row_speeds(first, rows):
    return speeds(first + lax.broadcasted_iota(jnp.int32, (rows, 1), 0))


def vert_plan(me, count, chunks):
    if count == 4:
        x, y = lax.rem(me, 2), lax.div(me, 2)
        px, py, pd = y * 2 + (1 - x), (1 - y) * 2 + x, 3 - me
        half = chunks // 2
        first = list(range(half))
        second = list(range(half, chunks))
        to_x = [(c, px, me, c) for c in first + second]
        to_y = [(chunks + c, py, me, c) for c in second + first]
        own = [send for pair in zip(to_x, to_y) for send in pair]
        from_x = [(c, px, c) for c in first + second]
        from_y = [(chunks + c, py, c) for c in second + first]
        arrivals = [item for pair in zip(from_x, from_y) for item in pair]
        forwards = {}
        for c in first:
            forwards[c] = (2 * chunks + c, py, px, c)
        for c in second:
            forwards[chunks + c] = (2 * chunks + c, px, py, c)
        late = [c for pair in zip(first, second) for c in pair]
        arrivals += [(2 * chunks + c, pd, c) for c in late]
        return own, arrivals, forwards
    own, arrivals = [], []
    for p in range(1, count):
        for c in range(chunks):
            key = (p - 1) * chunks + c
            own.append((key, lax.rem(me + p, count), me, c))
            arrivals.append((key, lax.rem(me + count - p, count), c))
    return own, arrivals, {}


def kernel(
    count, slabs, cols_ref, tiles_ref, dist_ref, relax_ref, weight_ref, out_ref,
    tiles, dense, source_rows, relax, node_weight, state, acc, gathered, plane_out, plane_in,
    mom_out, mom_in, gram_out, gram_in, weights2, tile_sem, source_sem, small_sem, vert_send,
    vert_recv, plane_send, plane_recv, mom_send, mom_recv, gram_send, gram_recv,
):
    rows, cells = state.shape
    lanes = cells // HALVES
    chunks = rows // CHUNK
    row_blocks = rows // TILE
    listed = tiles_ref.shape[2] // TILE
    me = lax.axis_index("vert")
    slab = lax.axis_index("gx")
    above = lax.rem(slab + 1, slabs)
    below = lax.rem(slab + slabs - 1, slabs)
    first_node = me * rows

    barrier = pltpu.get_barrier_semaphore()
    for p in range(1, count):
        pl.semaphore_signal(
            barrier, inc=1, device_id=(slab, lax.rem(me + p, count)), device_id_type=MESH
        )
    for other in (below, above):
        pl.semaphore_signal(barrier, inc=1, device_id=(other, me), device_id_type=MESH)

    source_loads = []
    for c in range(chunks):
        span = pl.ds(HALVES * CHUNK * c, HALVES * CHUNK)
        source_loads.append(
            pltpu.make_async_copy(dist_ref.at[span, :], source_rows.at[span, :], source_sem.at[c])
        )
    small_loads = [
        pltpu.make_async_copy(weight_ref, node_weight, small_sem.at[0]),
        pltpu.make_async_copy(relax_ref, relax, small_sem.at[1]),
    ]
    loads = [
        pltpu.make_async_copy(
            tiles_ref.at[:, :, pl.ds(j * TILE, TILE)], tiles.at[j], tile_sem.at[j]
        )
        for j in range(listed)
    ]
    for load in source_loads + small_loads + loads:
        load.start()

    own, arrivals, forwards = vert_plan(me, count, chunks)
    early = [item for item in arrivals if item[0] in forwards]
    rest = [item for item in arrivals if item[0] not in forwards]
    pending = []

    def vert_copy(stage, key, target, block, chunk):
        where = gathered.at[stage, block * chunks + chunk]
        return pltpu.make_async_remote_copy(
            src_ref=where, dst_ref=where, send_sem=vert_send.at[stage, key],
            recv_sem=vert_recv.at[stage, key], device_id=(slab, target), device_id_type=MESH,
        )

    def plane_copy(stage, side):
        return pltpu.make_async_remote_copy(
            src_ref=plane_out.at[stage, side], dst_ref=plane_in.at[stage, side],
            send_sem=plane_send.at[stage, side], recv_sem=plane_recv.at[stage, side],
            device_id=(above if side == 1 else below, me), device_id_type=MESH,
        )

    def mom_copy(stage, p):
        return pltpu.make_async_remote_copy(
            src_ref=mom_out.at[stage], dst_ref=mom_in.at[stage, p - 1],
            send_sem=mom_send.at[stage, p - 1], recv_sem=mom_recv.at[stage, p - 1],
            device_id=(slab, lax.rem(me + p, count)), device_id_type=MESH,
        )

    def gram_copy(p):
        return pltpu.make_async_remote_copy(
            src_ref=gram_out, dst_ref=gram_in.at[p - 1],
            send_sem=gram_send.at[p - 1], recv_sem=gram_recv.at[p - 1],
            device_id=(slab, lax.rem(me + p, count)), device_id_type=MESH,
        )

    def start(copy):
        copy.start()
        pending.append(copy)

    def publish(stage, base, part):
        chunk, inner = base // CHUNK, base % CHUNK
        gathered[stage, me * chunks + chunk, pl.ds(inner, PART), :] = part.astype(BF16)
        groups = part.reshape(PART // Q, 2, Q // 2, lanes)
        for side in range(2):
            plane_out[stage, side, pl.ds(base // 2, PART // 2), :] = (
                groups[:, side].reshape(PART // 2, lanes).astype(BF16)
            )

    def send_own(stage):
        for item in own:
            start(vert_copy(stage, *item))

    def send_planes(stage):
        for side in range(2):
            start(plane_copy(stage, side))

    for base in range(0, rows, PART):
        if base % CHUNK == 0:
            source_loads[base // CHUNK].wait()
        for half in range(HALVES):
            part = source_rows[pl.ds(HALVES * base + half, PART, stride=HALVES), :]
            state[pl.ds(base, PART), pl.ds(half * lanes, lanes)] = part
            publish(half, base, part)
    pl.semaphore_wait(barrier, count + 1)
    send_own(0)
    for half in range(HALVES):
        send_planes(half)

    for load in small_loads:
        load.wait()
    lane_node = first_node + lax.broadcasted_iota(jnp.int32, (8, rows), 1)
    kind = lax.broadcasted_iota(jnp.int32, (8, rows), 0)
    sx, sy, sz = speeds(lane_node)
    kinds = [jnp.ones_like(sx), sx, sy, sz, sx * sx + sy * sy + sz * sz]
    invariants = jnp.zeros_like(sx)
    for k, row in enumerate(kinds):
        invariants = jnp.where(kind == k, row, invariants)
    weighted = invariants * node_weight[...]
    high = weighted.astype(BF16).astype(F32)
    weights2[...] = jnp.concatenate([high, weighted - high], axis=0).astype(BF16)
    for l in range(5):
        column = jnp.sum(weighted * kinds[l], axis=1, keepdims=True)
        gram_out[l] = jnp.broadcast_to(column, (8, lanes))
    for p in range(1, count):
        start(gram_copy(p))

    tiles[listed] = jnp.zeros((row_blocks, TILE, TILE), BF16)
    for load in loads:
        load.wait()
    per_chunk = CHUNK // TILE

    def expand(r, carry):
        columns = [cols_ref[r, j] for j in range(listed)]
        here = pl.ds(pl.multiple_of(r * TILE, TILE), TILE)
        for c in range(RBLK):
            place = listed
            for j in range(listed):
                place = jnp.where(columns[j] == c, j, place)
            dense[c // per_chunk, here, pl.ds(c % per_chunk * TILE, TILE)] = tiles[place, r]
        return carry

    lax.fori_loop(0, row_blocks, expand, 0)

    def advect(step):
        for half in range(HALVES):
            for side in range(2):
                plane_copy(step * HALVES + half, side).wait_recv()

        def one(i, carry):
            base = pl.multiple_of(i * PART, PART)
            source = state[pl.ds(base, PART), :]
            planes = pl.ds(pl.multiple_of(i * (PART // 2), PART // 2), PART // 2)
            sides = [
                jnp.concatenate(
                    [plane_in[step * HALVES + half, side, planes, :] for half in range(HALVES)],
                    axis=1,
                ).astype(F32).reshape(PART // Q, 1, Q // 2, cells)
                for side in range(2)
            ]
            upwind_x = jnp.concatenate(sides, axis=1).reshape(PART, cells)
            px, py, pz = [COURANT_SCALE * s for s in row_speeds(first_node + base, PART)]
            z_index = lax.broadcasted_iota(jnp.int32, (PART, cells), 1) & (NZ - 1)
            lower_y = pltpu.roll(source, NZ, 1)
            upper_y = pltpu.roll(source, cells - NZ, 1)
            lower_z = jnp.where(
                z_index == 0, pltpu.roll(source, cells + 1 - NZ, 1), pltpu.roll(source, 1, 1)
            )
            upper_z = jnp.where(
                z_index == NZ - 1, pltpu.roll(source, NZ - 1, 1), pltpu.roll(source, cells - 1, 1)
            )
            flux = jnp.abs(px) * (source - upwind_x)
            flux += jnp.maximum(py, 0.0) * (source - lower_y) + jnp.minimum(py, 0.0) * (
                upper_y - source
            )
            flux += jnp.maximum(pz, 0.0) * (source - lower_z) + jnp.minimum(pz, 0.0) * (
                upper_z - source
            )
            acc[pl.ds(base, PART), :] = source - flux
            return carry

        lax.fori_loop(0, rows // PART, one, 0)

    def multiply(stage, index):
        side = pl.ds(stage % HALVES * lanes, lanes)

        def one(i, carry):
            here = pl.ds(pl.multiple_of(i * CHUNK, CHUNK), CHUNK)
            acc[here, side] += KERNEL_STEP * jnp.dot(
                dense[index, here, :], gathered[stage, index], preferred_element_type=F32
            )
            return carry

        lax.fori_loop(0, rows // CHUNK, one, 0, unroll=True)

    def arrive(stage, item):
        key, block, chunk = item
        vert_copy(stage, key, me, block, chunk).wait_recv()
        if key in forwards:
            start(vert_copy(stage, *forwards[key]))

    def relay(stage):
        for item in early:
            arrive(stage, item)

    def collide(stage):
        for chunk in range(chunks):
            multiply(stage, me * chunks + chunk)
        for key, block, chunk in early:
            multiply(stage, block * chunks + chunk)
        for item in rest:
            arrive(stage, item)
            multiply(stage, item[1] * chunks + item[2])
        side = pl.ds(stage % HALVES * lanes, lanes)
        total = jnp.zeros((16, lanes), F32)
        for base in range(0, rows, CHUNK):
            explicit = acc[pl.ds(base, CHUNK), side]
            top = explicit.astype(BF16)
            low = (explicit - top.astype(F32)).astype(BF16)
            left = weights2[:, pl.ds(base, CHUNK)]
            total += jnp.dot(left, top, preferred_element_type=F32)
            total += jnp.dot(left, low, preferred_element_type=F32)
        mom_out[stage] = total[:8] + total[8:]
        for p in range(1, count):
            start(mom_copy(stage, p))

    def invert():
        gram = gram_out[...]
        for p in range(1, count):
            gram_copy(p).wait_recv()
            gram += gram_in[p - 1]
        matrix = [[gram[l, k : k + 1, :] for l in range(5)] for k in range(5)]
        one, none = jnp.ones((1, lanes), F32), jnp.zeros((1, lanes), F32)
        inverse = [[one if k == l else none for l in range(5)] for k in range(5)]
        for k in range(5):
            scale = 1.0 / matrix[k][k]
            matrix[k] = [entry * scale for entry in matrix[k]]
            inverse[k] = [entry * scale for entry in inverse[k]]
            for r in range(5):
                if r != k:
                    factor = matrix[r][k]
                    matrix[r] = [a - factor * b for a, b in zip(matrix[r], matrix[k])]
                    inverse[r] = [a - factor * b for a, b in zip(inverse[r], inverse[k])]
        return inverse

    def relax_half(stage, inverse):
        half = stage % HALVES
        side = pl.ds(half * lanes, lanes)
        rate = relax[:, side]
        share = rate / (1.0 + rate)
        moments = mom_out[stage]
        for p in range(1, count):
            mom_copy(stage, p).wait_recv()
            moments += mom_in[stage, p - 1]
        coeffs = [
            share * sum(inverse[k][l] * moments[l : l + 1, :] for l in range(5)) for k in range(5)
        ]
        keep = 1.0 - share
        for base in range(0, rows, PART):
            vx, vy, vz = row_speeds(first_node + base, PART)
            squares = vx * vx + vy * vy + vz * vz
            equilibrium = (
                coeffs[0] + vx * coeffs[1] + vy * coeffs[2] + vz * coeffs[3] + squares * coeffs[4]
            )
            part = keep * acc[pl.ds(base, PART), side] + equilibrium
            if stage + HALVES < STEPS * HALVES:
                state[pl.ds(base, PART), side] = part
                publish(stage + HALVES, base, part)
            else:
                out_ref[pl.ds(HALVES * base + half, PART, stride=HALVES), :] = part
        if stage + HALVES < STEPS * HALVES:
            send_own(stage + HALVES)
            send_planes(stage + HALVES)

    advect(0)
    inverse = invert()
    relay(0)
    send_own(1)
    collide(0)
    relay(1)
    relax_half(0, inverse)
    collide(1)
    relay(2)
    relax_half(1, inverse)
    advect(1)
    collide(2)
    relay(3)
    relax_half(2, inverse)
    collide(3)
    relax_half(3, inverse)

    for copy in pending:
        copy.wait_send()


def per_device(count, slabs, distribution, relax_rate, node_weight, kernel_tiles, tile_cols):
    rows, depth, cells = distribution.shape
    assert depth == 1 and cells == 256 and rows % CHUNK == 0
    row_blocks, listed = tile_cols.shape
    chunks = rows // CHUNK
    keys = 3 * chunks if count == 4 else (count - 1) * chunks
    peers = count - 1
    stages = STEPS * HALVES
    lanes = cells // HALVES
    vmem = pl.BlockSpec(memory_space=pltpu.VMEM)
    dma = pltpu.SemaphoreType.DMA
    result = pl.pallas_call(
        functools.partial(kernel, count, slabs),
        out_shape=jax.ShapeDtypeStruct((rows * HALVES, lanes), F32),
        in_specs=[pl.BlockSpec(memory_space=pltpu.SMEM)] + [pl.BlockSpec(memory_space=pltpu.HBM)] * 4,
        out_specs=vmem,
        scratch_shapes=[
            pltpu.VMEM((listed + 1, row_blocks, TILE, TILE), BF16),
            pltpu.VMEM((V // CHUNK, rows, CHUNK), BF16),
            pltpu.VMEM((rows * HALVES, lanes), F32),
            pltpu.VMEM((1, cells), F32),
            pltpu.VMEM((1, rows), F32),
            pltpu.VMEM((rows, cells), F32),
            pltpu.VMEM((rows, cells), F32),
            pltpu.VMEM((stages, V // CHUNK, CHUNK, lanes), BF16),
            pltpu.VMEM((stages, 2, rows // 2, lanes), BF16),
            pltpu.VMEM((stages, 2, rows // 2, lanes), BF16),
            pltpu.VMEM((stages, 8, lanes), F32),
            pltpu.VMEM((stages, peers, 8, lanes), F32),
            pltpu.VMEM((5, 8, lanes), F32),
            pltpu.VMEM((peers, 5, 8, lanes), F32),
            pltpu.VMEM((16, rows), BF16),
            dma((listed,)),
            dma((chunks,)),
            dma((2,)),
            dma((stages, keys)),
            dma((stages, keys)),
            dma((stages, 2)),
            dma((stages, 2)),
            dma((stages, peers)),
            dma((stages, peers)),
            dma((peers,)),
            dma((peers,)),
        ],
        compiler_params=pltpu.CompilerParams(
            collective_id=0, has_side_effects=True, vmem_limit_bytes=63 * 1024 * 1024
        ),
        name="bgk_steps",
    )(
        tile_cols, kernel_tiles, distribution.reshape(rows * HALVES, lanes), relax_rate,
        node_weight.reshape(1, rows),
    )
    return result.reshape(rows, depth, cells)


def solution(mesh):
    placed = (
        P("vert", "gx", None),
        P("gx", None),
        P("vert"),
        P("vert", None, None),
        P("vert", None),
    )
    return jax.shard_map(
        functools.partial(per_device, mesh.shape["vert"], mesh.shape["gx"]),
        mesh=mesh, in_specs=placed, out_specs=P("vert", "gx", None), check_vma=False,
    )
```

time: 58.5 us -> 61.1 us (1.044)
  Pallas kernels: 51.9 us -> 57.9 us
  local copies, waits for them, and re-layouts: 6.21 us -> 2.91 us
    pallas_call x1, Pallas kernels: 51.9 us -> 57.9 us  [per_device(): pl.pallas_call(functools.partial(kernel, count, slabs), out_shape=jax.Sha...]
    unnamed x10 -> x1, local copies, waits for them, and re-layouts: 6.21 us -> 2.91 us
where the time goes in v2:
time: 61.1 us; the launch traced here: 60.9 us
  Pallas kernels  57.9 us (95%)
  local copies, waits for them, and re-layouts  2.91 us (5%)
    pallas_call x1, Pallas kernels, per_device(): pl.pallas_call(functools.partial(kernel, count, slabs), out_shape=jax.Sha...  57.9 us
    unnamed x1, local copies, waits for them, and re-layouts  2.91 us

profile of v2, /device:TPU:0, one launch (start us, length us, event | category | flops | bytes accessed | tf_op | source)
XLA Modules:
  0.0 60.9 jit_solution(4002863382721497657)
XLA Ops:
  0.0 57.9 %bgk_steps.1 = f32[2048,128]{1,0:T(8,128)} custom-call(s32[8,12]{1,0:T(8,128)} %cols_ref.1, bf16[8,128,1536]{2,1,0:T(8,128)(2,1)} %tiles_ref.1, f32[2048,128]{1,0:T(8,128)} %bitcast.4, f32[1,256]{1,0:T(1,128)} %relax_ref.1, f32[1,1024]{1,0:T(1,128)} %bitcast.5), custom_call_target="tpu_custom_call" | custom-call | tf_op jit(solution)/shard_map/bgk_steps/pallas_call | solution.py:375
  58.0 2.9 %copy.8 = f32[1024,1,256]{2,1,0:T(1,128)} copy(f32[1024,1,256]{2,1,0:T(1,128)} %bitcast.3) | data formatting | bytes 2097152

commit v3 on v2

--- a/solution.py
+++ b/solution.py
@@ -66,7 +66,7 @@
 
 
 def kernel(
-    count, slabs, cols_ref, tiles_ref, dist_ref, relax_ref, weight_ref, out_ref,
+    count, slabs, cols_ref, tiles_ref, dist_ref, relax_ref, weight_ref, out_ref, constant_ref,
     tiles, dense, source_rows, relax, node_weight, state, acc, gathered, plane_out, plane_in,
     mom_out, mom_in, gram_out, gram_in, weights2, tile_sem, source_sem, small_sem, vert_send,
     vert_recv, plane_send, plane_recv, mom_send, mom_recv, gram_send, gram_recv,
@@ -146,33 +146,40 @@
         copy.start()
         pending.append(copy)
 
-    def publish(stage, base, part):
+    def publish_block(stage, base, part):
         chunk, inner = base // CHUNK, base % CHUNK
         gathered[stage, me * chunks + chunk, pl.ds(inner, PART), :] = part.astype(BF16)
+
+    def publish_planes(stage, base, part):
         groups = part.reshape(PART // Q, 2, Q // 2, lanes)
         for side in range(2):
             plane_out[stage, side, pl.ds(base // 2, PART // 2), :] = (
                 groups[:, side].reshape(PART // 2, lanes).astype(BF16)
             )
 
-    def send_own(stage):
-        for item in own:
+    def send_own(stage, items=own):
+        for item in items:
             start(vert_copy(stage, *item))
 
     def send_planes(stage):
         for side in range(2):
             start(plane_copy(stage, side))
 
-    for base in range(0, rows, PART):
-        if base % CHUNK == 0:
-            source_loads[base // CHUNK].wait()
-        for half in range(HALVES):
+    for half in range(HALVES):
+        for base in range(0, rows, PART):
+            if half == 0 and base % CHUNK == 0:
+                source_loads[base // CHUNK].wait()
             part = source_rows[pl.ds(HALVES * base + half, PART, stride=HALVES), :]
             state[pl.ds(base, PART), pl.ds(half * lanes, lanes)] = part
-            publish(half, base, part)
-    pl.semaphore_wait(barrier, count + 1)
-    send_own(0)
+            publish_block(half, base, part)
+        if half == 0:
+            pl.semaphore_wait(barrier, count + 1)
+            send_own(0)
+        else:
+            send_own(1, own[: len(own) // 2])
     for half in range(HALVES):
+        for base in range(0, rows, PART):
+            publish_planes(half, base, state[pl.ds(base, PART), pl.ds(half * lanes, lanes)])
         send_planes(half)
 
     for load in small_loads:
@@ -249,14 +256,17 @@
 
         lax.fori_loop(0, rows // PART, one, 0)
 
-    def multiply(stage, index):
+    def multiply(stage, indices):
         side = pl.ds(stage % HALVES * lanes, lanes)
 
         def one(i, carry):
             here = pl.ds(pl.multiple_of(i * CHUNK, CHUNK), CHUNK)
-            acc[here, side] += KERNEL_STEP * jnp.dot(
-                dense[index, here, :], gathered[stage, index], preferred_element_type=F32
-            )
+            total = jnp.zeros((CHUNK, lanes), F32)
+            for index in indices:
+                total += jnp.dot(
+                    dense[index, here, :], gathered[stage, index], preferred_element_type=F32
+                )
+            acc[here, side] += KERNEL_STEP * total
             return carry
 
         lax.fori_loop(0, rows // CHUNK, one, 0, unroll=True)
@@ -272,13 +282,12 @@
             arrive(stage, item)
 
     def collide(stage):
-        for chunk in range(chunks):
-            multiply(stage, me * chunks + chunk)
-        for key, block, chunk in early:
-            multiply(stage, block * chunks + chunk)
-        for item in rest:
-            arrive(stage, item)
-            multiply(stage, item[1] * chunks + item[2])
+        ready = [me * chunks + chunk for chunk in range(chunks)]
+        multiply(stage, ready + [block * chunks + chunk for _, block, chunk in early])
+        for at in range(0, len(rest), 2):
+            for item in rest[at : at + 2]:
+                arrive(stage, item)
+            multiply(stage, [block * chunks + chunk for _, block, chunk in rest[at : at + 2]])
         side = pl.ds(stage % HALVES * lanes, lanes)
         total = jnp.zeros((16, lanes), F32)
         for base in range(0, rows, CHUNK):
@@ -324,28 +333,32 @@
             share * sum(inverse[k][l] * moments[l : l + 1, :] for l in range(5)) for k in range(5)
         ]
         keep = 1.0 - share
+        last = stage + HALVES >= STEPS * HALVES
+        if last:
+            constant_ref[:, side] = coeffs[0]
         for base in range(0, rows, PART):
             vx, vy, vz = row_speeds(first_node + base, PART)
             squares = vx * vx + vy * vy + vz * vz
-            equilibrium = (
-                coeffs[0] + vx * coeffs[1] + vy * coeffs[2] + vz * coeffs[3] + squares * coeffs[4]
-            )
-            part = keep * acc[pl.ds(base, PART), side] + equilibrium
-            if stage + HALVES < STEPS * HALVES:
+            part = keep * acc[pl.ds(base, PART), side]
+            part += vx * coeffs[1] + vy * coeffs[2] + vz * coeffs[3] + squares * coeffs[4]
+            if last:
+                out_ref[pl.ds(HALVES * base + half, PART, stride=HALVES), :] = part
+            else:
+                part += coeffs[0]
                 state[pl.ds(base, PART), side] = part
-                publish(stage + HALVES, base, part)
-            else:
-                out_ref[pl.ds(HALVES * base + half, PART, stride=HALVES), :] = part
-        if stage + HALVES < STEPS * HALVES:
+                publish_block(stage + HALVES, base, part)
+        if not last:
             send_own(stage + HALVES)
+            for base in range(0, rows, PART):
+                publish_planes(stage + HALVES, base, state[pl.ds(base, PART), side])
             send_planes(stage + HALVES)
 
+    relay(0)
+    send_own(1, own[len(own) // 2 :])
     advect(0)
-    inverse = invert()
-    relay(0)
-    send_own(1)
     collide(0)
     relay(1)
+    inverse = invert()
     relax_half(0, inverse)
     collide(1)
     relay(2)
@@ -372,11 +385,14 @@
     lanes = cells // HALVES
     vmem = pl.BlockSpec(memory_space=pltpu.VMEM)
     dma = pltpu.SemaphoreType.DMA
-    result = pl.pallas_call(
+    result, constant = pl.pallas_call(
         functools.partial(kernel, count, slabs),
-        out_shape=jax.ShapeDtypeStruct((rows * HALVES, lanes), F32),
+        out_shape=(
+            jax.ShapeDtypeStruct((rows * HALVES, lanes), F32),
+            jax.ShapeDtypeStruct((1, cells), F32),
+        ),
         in_specs=[pl.BlockSpec(memory_space=pltpu.SMEM)] + [pl.BlockSpec(memory_space=pltpu.HBM)] * 4,
-        out_specs=vmem,
+        out_specs=(vmem, vmem),
         scratch_shapes=[
             pltpu.VMEM((listed + 1, row_blocks, TILE, TILE), BF16),
             pltpu.VMEM((V // CHUNK, rows, CHUNK), BF16),
@@ -413,7 +429,7 @@
         tile_cols, kernel_tiles, distribution.reshape(rows * HALVES, lanes), relax_rate,
         node_weight.reshape(1, rows),
     )
-    return result.reshape(rows, depth, cells)
+    return result.reshape(rows, depth, cells) + constant[None]
 
 
 def solution(mesh):

time: 61.1 us -> 56.6 us (0.926)
  Pallas kernels: 57.9 us -> 53.5 us
  other arithmetic: 0 us -> 2.92 us
  local copies, waits for them, and re-layouts: 2.91 us -> 0 us
    pallas_call x1, Pallas kernels: 57.9 us -> 53.5 us  [per_device(): pl.pallas_call(functools.partial(kernel, count, slabs), out_shape=(jax.Sh...]
    add x0 -> x1, other arithmetic: none -> 2.92 us  [per_device(): return result.reshape(rows, depth, cells) + constant[None]]
    unnamed x1 -> x0, local copies, waits for them, and re-layouts: 2.91 us -> none
where the time goes in v3:
time: 56.6 us; the launch traced here: 56.4 us
  Pallas kernels  53.5 us (95%)
  other arithmetic  2.92 us (5%)
    pallas_call x1, Pallas kernels, per_device(): pl.pallas_call(functools.partial(kernel, count, slabs), out_shape=(jax.Sh...  53.5 us
    add x1, other arithmetic, per_device(): return result.reshape(rows, depth, cells) + constant[None]  2.92 us

profile of v3, /device:TPU:0, one launch (start us, length us, event | category | flops | bytes accessed | tf_op | source)
XLA Modules:
  0.0 56.4 jit_solution(4819427146215163906)
XLA Ops:
  0.0 53.5 %bgk_steps.1 = (f32[2048,128]{1,0:T(8,128)}, f32[1,256]{1,0:T(1,128)}) custom-call(s32[8,12]{1,0:T(8,128)} %cols_ref.1, bf16[8,128,1536]{2,1,0:T(8,128)(2,1)} %tiles_ref.1, f32[2048,128]{1,0:T(8,128)} %bitcast.4, f32[1,256]{1,0:T(1,128)} %relax_ref.1, f32[1,1024]{1,0:T(1,128)} %bitcast.6), custom_call_target="tpu_custom_call" | custom-call | tf_op jit(solution)/shard_map/bgk_steps/pallas_call | solution.py:388
  53.5 2.9 %broadcast_add_fusion = f32[1024,1,256]{2,1,0:T(1,128)} fusion(f32[1024,1,256]{2,1,0:T(1,128)} %bitcast.5, f32[256]{0:T(256)} %bitcast.7), kind=kLoop, calls=%fused_computation | loop fusion | flops 262144 | bytes 2098176 | tf_op jit(solution)/shard_map/add | solution.py:432

commit v4 on v3

--- a/solution.py
+++ b/solution.py
@@ -68,7 +68,8 @@
 def kernel(
     count, slabs, cols_ref, tiles_ref, dist_ref, relax_ref, weight_ref, out_ref, constant_ref,
     tiles, dense, source_rows, relax, node_weight, state, acc, gathered, plane_out, plane_in,
-    mom_out, mom_in, gram_out, gram_in, weights2, tile_sem, source_sem, small_sem, vert_send,
+    mom_out, mom_in, gram_out, gram_in, weights2,
+    spread, node_table, coeff_rows, tile_sem, source_sem, small_sem, vert_send,
     vert_recv, plane_send, plane_recv, mom_send, mom_recv, gram_send, gram_recv,
 ):
     rows, cells = state.shape
@@ -251,12 +252,21 @@
             flux += jnp.maximum(pz, 0.0) * (source - lower_z) + jnp.minimum(pz, 0.0) * (
                 upper_z - source
             )
-            acc[pl.ds(base, PART), :] = source - flux
+            if step == 0:
+                acc[pl.ds(base, PART), :] = source - flux
+            else:
+                shift = jnp.dot(
+                    spread[pl.ds(base, PART), :], coeff_rows[...],
+                    precision=lax.Precision.HIGHEST, preferred_element_type=F32,
+                )
+                result = source - flux + shift
+                acc[pl.ds(base, PART), pl.ds(0, lanes)] += result[:, :lanes]
+                acc[pl.ds(base, PART), pl.ds(lanes, cells - lanes)] = result[:, lanes:]
             return carry
 
         lax.fori_loop(0, rows // PART, one, 0)
 
-    def multiply(stage, indices):
+    def multiply(stage, indices, fresh=False):
         side = pl.ds(stage % HALVES * lanes, lanes)
 
         def one(i, carry):
@@ -266,7 +276,10 @@
                 total += jnp.dot(
                     dense[index, here, :], gathered[stage, index], preferred_element_type=F32
                 )
-            acc[here, side] += KERNEL_STEP * total
+            if fresh:
+                acc[here, side] = KERNEL_STEP * total
+            else:
+                acc[here, side] += KERNEL_STEP * total
             return carry
 
         lax.fori_loop(0, rows // CHUNK, one, 0, unroll=True)
@@ -281,13 +294,15 @@
         for item in early:
             arrive(stage, item)
 
-    def collide(stage):
+    def kernel_term(stage, fresh=False):
         ready = [me * chunks + chunk for chunk in range(chunks)]
-        multiply(stage, ready + [block * chunks + chunk for _, block, chunk in early])
+        multiply(stage, ready + [block * chunks + chunk for _, block, chunk in early], fresh)
         for at in range(0, len(rest), 2):
             for item in rest[at : at + 2]:
                 arrive(stage, item)
             multiply(stage, [block * chunks + chunk for _, block, chunk in rest[at : at + 2]])
+
+    def send_moments(stage):
         side = pl.ds(stage % HALVES * lanes, lanes)
         total = jnp.zeros((16, lanes), F32)
         for base in range(0, rows, CHUNK):
@@ -300,6 +315,43 @@
         mom_out[stage] = total[:8] + total[8:]
         for p in range(1, count):
             start(mom_copy(stage, p))
+
+    def spread_invariants():
+        lane = lax.broadcasted_iota(jnp.int32, (CHUNK, TILE), 1)
+        node = lax.broadcasted_iota(jnp.int32, (CHUNK, TILE), 0)
+        which = lane & 7
+        tx, ty, _ = speeds(node)
+        flat = jnp.where(which == 0, 1.0, 0.0)
+        flat = jnp.where(which == 1, tx, jnp.where(which == 2, ty, flat))
+        flat = jnp.where(which == 4, tx * tx + ty * ty, flat)
+        first_z = jnp.where(which == 3, 1.0, 0.0)
+        second_z = jnp.where(which == 4, 1.0, 0.0)
+        middle = (Q - 1) / 2.0
+        for k in range(V // CHUNK):
+            tz = (k - middle) / middle
+            table = flat + tz * first_z + (tz * tz) * second_z
+            top = table.astype(BF16).astype(F32)
+            table = jnp.where(lane < 8, top, jnp.where(lane < 16, table - top, 0.0))
+            node_table[k] = table.astype(BF16)
+
+        def one(i, carry):
+            here = pl.ds(pl.multiple_of(i * CHUNK, CHUNK), CHUNK)
+            total = jnp.zeros((CHUNK, TILE), F32)
+            for k in range(V // CHUNK):
+                total += jnp.dot(
+                    dense[k, here, :], node_table[k], preferred_element_type=F32
+                )
+            spread[here, :] = total
+            return carry
+
+        lax.fori_loop(0, rows // CHUNK, one, 0)
+
+    def publish_scaled(stage):
+        side = pl.ds(stage % HALVES * lanes, lanes)
+        keep = 1.0 / (1.0 + relax[:, side])
+        for base in range(0, rows, PART):
+            publish_block(stage + HALVES, base, keep * acc[pl.ds(base, PART), side])
+        send_own(stage + HALVES)
 
     def invert():
         gram = gram_out[...]
@@ -336,6 +388,10 @@
         last = stage + HALVES >= STEPS * HALVES
         if last:
             constant_ref[:, side] = coeffs[0]
+        else:
+            for k in range(5):
+                for row in (k, k + 8):
+                    coeff_rows[row : row + 1, side] = KERNEL_STEP * coeffs[k]
         for base in range(0, rows, PART):
             vx, vy, vz = row_speeds(first_node + base, PART)
             squares = vx * vx + vy * vy + vz * vz
@@ -346,28 +402,33 @@
             else:
                 part += coeffs[0]
                 state[pl.ds(base, PART), side] = part
-                publish_block(stage + HALVES, base, part)
+                publish_planes(stage + HALVES, base, part)
         if not last:
-            send_own(stage + HALVES)
-            for base in range(0, rows, PART):
-                publish_planes(stage + HALVES, base, state[pl.ds(base, PART), side])
             send_planes(stage + HALVES)
 
     relay(0)
     send_own(1, own[len(own) // 2 :])
     advect(0)
-    collide(0)
+    kernel_term(0)
+    publish_scaled(0)
     relay(1)
+    send_moments(0)
+    kernel_term(1)
+    publish_scaled(1)
+    send_moments(1)
+    coeff_rows[...] = jnp.zeros(coeff_rows.shape, F32)
+    spread_invariants()
+    relay(2)
     inverse = invert()
     relax_half(0, inverse)
-    collide(1)
-    relay(2)
     relax_half(1, inverse)
+    kernel_term(2, fresh=True)
+    relay(3)
     advect(1)
-    collide(2)
-    relay(3)
+    send_moments(2)
+    kernel_term(3)
+    send_moments(3)
     relax_half(2, inverse)
-    collide(3)
     relax_half(3, inverse)
 
     for copy in pending:
@@ -409,6 +470,9 @@
             pltpu.VMEM((5, 8, lanes), F32),
             pltpu.VMEM((peers, 5, 8, lanes), F32),
             pltpu.VMEM((16, rows), BF16),
+            pltpu.VMEM((rows, TILE), F32),
+            pltpu.VMEM((V // CHUNK, CHUNK, TILE), BF16),
+            pltpu.VMEM((TILE, cells), F32),
             dma((listed,)),
             dma((chunks,)),
             dma((2,)),

time: 56.6 us -> 58 us (1.025)
  Pallas kernels: 53.5 us -> 54.9 us
    pallas_call x1, Pallas kernels: 53.5 us -> 54.9 us  [per_device(): pl.pallas_call(functools.partial(kernel, count, slabs), out_shape=(jax.Sh...]
where the time goes in v4:
time: 58 us; the launch traced here: 57.9 us
  Pallas kernels  54.9 us (95%)
  other arithmetic  2.92 us (5%)
    pallas_call x1, Pallas kernels, per_device(): pl.pallas_call(functools.partial(kernel, count, slabs), out_shape=(jax.Sh...  54.9 us
    add x1, other arithmetic, per_device(): return result.reshape(rows, depth, cells) + constant[None]  2.92 us

profile of v4, /device:TPU:0, one launch (start us, length us, event | category | flops | bytes accessed | tf_op | source)
XLA Modules:
  0.0 57.9 jit_solution(16281194877983103485)
XLA Ops:
  0.0 54.9 %bgk_steps.1 = (f32[2048,128]{1,0:T(8,128)}, f32[1,256]{1,0:T(1,128)}) custom-call(s32[8,12]{1,0:T(8,128)} %cols_ref.1, bf16[8,128,1536]{2,1,0:T(8,128)(2,1)} %tiles_ref.1, f32[2048,128]{1,0:T(8,128)} %bitcast.4, f32[1,256]{1,0:T(1,128)} %relax_ref.1, f32[1,1024]{1,0:T(1,128)} %bitcast.6), custom_call_target="tpu_custom_call" | custom-call | tf_op jit(solution)/shard_map/bgk_steps/pallas_call | solution.py:449
  54.9 2.9 %broadcast_add_fusion = f32[1024,1,256]{2,1,0:T(1,128)} fusion(f32[1024,1,256]{2,1,0:T(1,128)} %bitcast.5, f32[256]{0:T(256)} %bitcast.7), kind=kLoop, calls=%fused_computation | loop fusion | flops 262144 | bytes 2098176 | tf_op jit(solution)/shard_map/add | solution.py:496

commit v5 on v4

--- a/solution.py
+++ b/solution.py
@@ -11,7 +11,8 @@
 TILE = 128
 NZ = 4
 STEPS = 2
-HALVES = 2
+HALVES = 1
+SPLIT = 2
 V = 4096
 RBLK = 32
 CHUNK = 256
@@ -53,7 +54,7 @@
             forwards[c] = (2 * chunks + c, py, px, c)
         for c in second:
             forwards[chunks + c] = (2 * chunks + c, px, py, c)
-        late = [c for pair in zip(first, second) for c in pair]
+        late = first + second
         arrivals += [(2 * chunks + c, pd, c) for c in late]
         return own, arrivals, forwards
     own, arrivals = [], []
@@ -93,7 +94,7 @@
 
     source_loads = []
     for c in range(chunks):
-        span = pl.ds(HALVES * CHUNK * c, HALVES * CHUNK)
+        span = pl.ds(SPLIT * CHUNK * c, SPLIT * CHUNK)
         source_loads.append(
             pltpu.make_async_copy(dist_ref.at[span, :], source_rows.at[span, :], source_sem.at[c])
         )
@@ -116,7 +117,7 @@
     pending = []
 
     def vert_copy(stage, key, target, block, chunk):
-        where = gathered.at[stage, block * chunks + chunk]
+        where = gathered.at[stage, block, pl.ds(chunk * CHUNK, CHUNK), :]
         return pltpu.make_async_remote_copy(
             src_ref=where, dst_ref=where, send_sem=vert_send.at[stage, key],
             recv_sem=vert_recv.at[stage, key], device_id=(slab, target), device_id_type=MESH,
@@ -148,8 +149,7 @@
         pending.append(copy)
 
     def publish_block(stage, base, part):
-        chunk, inner = base // CHUNK, base % CHUNK
-        gathered[stage, me * chunks + chunk, pl.ds(inner, PART), :] = part.astype(BF16)
+        gathered[stage, me, pl.ds(base, PART), :] = part.astype(BF16)
 
     def publish_planes(stage, base, part):
         groups = part.reshape(PART // Q, 2, Q // 2, lanes)
@@ -166,22 +166,21 @@
         for side in range(2):
             start(plane_copy(stage, side))
 
-    for half in range(HALVES):
-        for base in range(0, rows, PART):
-            if half == 0 and base % CHUNK == 0:
-                source_loads[base // CHUNK].wait()
-            part = source_rows[pl.ds(HALVES * base + half, PART, stride=HALVES), :]
-            state[pl.ds(base, PART), pl.ds(half * lanes, lanes)] = part
-            publish_block(half, base, part)
-        if half == 0:
-            pl.semaphore_wait(barrier, count + 1)
-            send_own(0)
-        else:
-            send_own(1, own[: len(own) // 2])
-    for half in range(HALVES):
-        for base in range(0, rows, PART):
-            publish_planes(half, base, state[pl.ds(base, PART), pl.ds(half * lanes, lanes)])
-        send_planes(half)
+    for base in range(0, rows, PART):
+        if base % CHUNK == 0:
+            source_loads[base // CHUNK].wait()
+        pieces = [
+            source_rows[pl.ds(SPLIT * base + piece, PART, stride=SPLIT), :]
+            for piece in range(SPLIT)
+        ]
+        part = jnp.concatenate(pieces, axis=1)
+        state[pl.ds(base, PART), :] = part
+        publish_block(0, base, part)
+    pl.semaphore_wait(barrier, count + 1)
+    send_own(0)
+    for base in range(0, rows, PART):
+        publish_planes(0, base, state[pl.ds(base, PART), :])
+    send_planes(0)
 
     for load in small_loads:
         load.wait()
@@ -204,8 +203,6 @@
     tiles[listed] = jnp.zeros((row_blocks, TILE, TILE), BF16)
     for load in loads:
         load.wait()
-    per_chunk = CHUNK // TILE
-
     def expand(r, carry):
         columns = [cols_ref[r, j] for j in range(listed)]
         here = pl.ds(pl.multiple_of(r * TILE, TILE), TILE)
@@ -213,7 +210,7 @@
             place = listed
             for j in range(listed):
                 place = jnp.where(columns[j] == c, j, place)
-            dense[c // per_chunk, here, pl.ds(c % per_chunk * TILE, TILE)] = tiles[place, r]
+            dense[c // row_blocks, here, pl.ds(c % row_blocks * TILE, TILE)] = tiles[place, r]
         return carry
 
     lax.fori_loop(0, row_blocks, expand, 0)
@@ -259,30 +256,29 @@
                     spread[pl.ds(base, PART), :], coeff_rows[...],
                     precision=lax.Precision.HIGHEST, preferred_element_type=F32,
                 )
-                result = source - flux + shift
-                acc[pl.ds(base, PART), pl.ds(0, lanes)] += result[:, :lanes]
-                acc[pl.ds(base, PART), pl.ds(lanes, cells - lanes)] = result[:, lanes:]
+                acc[pl.ds(base, PART), :] += source - flux + shift
             return carry
 
         lax.fori_loop(0, rows // PART, one, 0)
 
-    def multiply(stage, indices, fresh=False):
-        side = pl.ds(stage % HALVES * lanes, lanes)
-
+    def multiply(stage, groups, fresh=False):
         def one(i, carry):
             here = pl.ds(pl.multiple_of(i * CHUNK, CHUNK), CHUNK)
-            total = jnp.zeros((CHUNK, lanes), F32)
-            for index in indices:
-                total += jnp.dot(
-                    dense[index, here, :], gathered[stage, index], preferred_element_type=F32
+            total = None
+            for block, first, length in groups:
+                span = pl.ds(first * CHUNK, length * CHUNK)
+                term = jnp.dot(
+                    dense[block, here, span], gathered[stage, block, span, :],
+                    preferred_element_type=F32,
                 )
+                total = term if total is None else total + term
             if fresh:
-                acc[here, side] = KERNEL_STEP * total
+                acc[here, :] = KERNEL_STEP * total
             else:
-                acc[here, side] += KERNEL_STEP * total
+                acc[here, :] += KERNEL_STEP * total
             return carry
 
-        lax.fori_loop(0, rows // CHUNK, one, 0, unroll=True)
+        lax.fori_loop(0, rows // CHUNK, one, 0)
 
     def arrive(stage, item):
         key, block, chunk = item
@@ -294,13 +290,24 @@
         for item in early:
             arrive(stage, item)
 
-    def kernel_term(stage, fresh=False):
-        ready = [me * chunks + chunk for chunk in range(chunks)]
-        multiply(stage, ready + [block * chunks + chunk for _, block, chunk in early], fresh)
-        for at in range(0, len(rest), 2):
-            for item in rest[at : at + 2]:
+    def runs(items):
+        found = {}
+        for _, block, chunk in items:
+            found.setdefault(id(block), (block, []))[1].append(chunk)
+        return [(block, min(held), len(held)) for block, held in found.values()]
+
+    def kernel_first(stage, fresh=False):
+        multiply(stage, [(me, 0, chunks)] + runs(early), fresh)
+
+    def kernel_rest(stage):
+        at = 0
+        while at < len(rest):
+            size = chunks if at < chunks or count != 4 else chunks // 2
+            part = rest[at : at + size]
+            for item in part:
                 arrive(stage, item)
-            multiply(stage, [block * chunks + chunk for _, block, chunk in rest[at : at + 2]])
+            multiply(stage, runs(part))
+            at += size
 
     def send_moments(stage):
         side = pl.ds(stage % HALVES * lanes, lanes)
@@ -339,7 +346,8 @@
             total = jnp.zeros((CHUNK, TILE), F32)
             for k in range(V // CHUNK):
                 total += jnp.dot(
-                    dense[k, here, :], node_table[k], preferred_element_type=F32
+                    dense[k // chunks, here, pl.ds(k % chunks * CHUNK, CHUNK)], node_table[k],
+                    preferred_element_type=F32,
                 )
             spread[here, :] = total
             return carry
@@ -373,8 +381,7 @@
         return inverse
 
     def relax_half(stage, inverse):
-        half = stage % HALVES
-        side = pl.ds(half * lanes, lanes)
+        side = pl.ds(0, lanes)
         rate = relax[:, side]
         share = rate / (1.0 + rate)
         moments = mom_out[stage]
@@ -398,7 +405,10 @@
             part = keep * acc[pl.ds(base, PART), side]
             part += vx * coeffs[1] + vy * coeffs[2] + vz * coeffs[3] + squares * coeffs[4]
             if last:
-                out_ref[pl.ds(HALVES * base + half, PART, stride=HALVES), :] = part
+                for piece in range(SPLIT):
+                    out_ref[pl.ds(SPLIT * base + piece, PART, stride=SPLIT), :] = part[
+                        :, piece * 128 : (piece + 1) * 128
+                    ]
             else:
                 part += coeffs[0]
                 state[pl.ds(base, PART), side] = part
@@ -407,29 +417,21 @@
             send_planes(stage + HALVES)
 
     relay(0)
-    send_own(1, own[len(own) // 2 :])
     advect(0)
-    kernel_term(0)
+    kernel_first(0)
+    kernel_rest(0)
     publish_scaled(0)
-    relay(1)
     send_moments(0)
-    kernel_term(1)
-    publish_scaled(1)
-    send_moments(1)
     coeff_rows[...] = jnp.zeros(coeff_rows.shape, F32)
     spread_invariants()
-    relay(2)
     inverse = invert()
     relax_half(0, inverse)
+    relay(1)
+    kernel_first(1, fresh=True)
+    advect(1)
+    kernel_rest(1)
+    send_moments(1)
     relax_half(1, inverse)
-    kernel_term(2, fresh=True)
-    relay(3)
-    advect(1)
-    send_moments(2)
-    kernel_term(3)
-    send_moments(3)
-    relax_half(2, inverse)
-    relax_half(3, inverse)
 
     for copy in pending:
         copy.wait_send()
@@ -449,20 +451,20 @@
     result, constant = pl.pallas_call(
         functools.partial(kernel, count, slabs),
         out_shape=(
-            jax.ShapeDtypeStruct((rows * HALVES, lanes), F32),
+            jax.ShapeDtypeStruct((rows * SPLIT, cells // SPLIT), F32),
             jax.ShapeDtypeStruct((1, cells), F32),
         ),
         in_specs=[pl.BlockSpec(memory_space=pltpu.SMEM)] + [pl.BlockSpec(memory_space=pltpu.HBM)] * 4,
         out_specs=(vmem, vmem),
         scratch_shapes=[
             pltpu.VMEM((listed + 1, row_blocks, TILE, TILE), BF16),
-            pltpu.VMEM((V // CHUNK, rows, CHUNK), BF16),
-            pltpu.VMEM((rows * HALVES, lanes), F32),
+            pltpu.VMEM((V // rows, rows, rows), BF16),
+            pltpu.VMEM((rows * SPLIT, cells // SPLIT), F32),
             pltpu.VMEM((1, cells), F32),
             pltpu.VMEM((1, rows), F32),
             pltpu.VMEM((rows, cells), F32),
             pltpu.VMEM((rows, cells), F32),
-            pltpu.VMEM((stages, V // CHUNK, CHUNK, lanes), BF16),
+            pltpu.VMEM((stages, V // rows, rows, lanes), BF16),
             pltpu.VMEM((stages, 2, rows // 2, lanes), BF16),
             pltpu.VMEM((stages, 2, rows // 2, lanes), BF16),
             pltpu.VMEM((stages, 8, lanes), F32),
@@ -490,7 +492,7 @@
         ),
         name="bgk_steps",
     )(
-        tile_cols, kernel_tiles, distribution.reshape(rows * HALVES, lanes), relax_rate,
+        tile_cols, kernel_tiles, distribution.reshape(rows * SPLIT, cells // SPLIT), relax_rate,
         node_weight.reshape(1, rows),
     )
     return result.reshape(rows, depth, cells) + constant[None]

time: 58 us -> 63 us (1.086); the launches traced: 57.9 us -> 62.1 us
  Pallas kernels: 54.9 us -> 59.2 us
    pallas_call x1, Pallas kernels: 54.9 us -> 59.2 us  [per_device(): pl.pallas_call(functools.partial(kernel, count, slabs), out_shape=(jax.Sh...]
where the time goes in v5:
time: 63 us; the launch traced here: 62.1 us
  Pallas kernels  59.2 us (94%)
  other arithmetic  2.92 us (5%)
    pallas_call x1, Pallas kernels, per_device(): pl.pallas_call(functools.partial(kernel, count, slabs), out_shape=(jax.Sh...  59.2 us
    add x1, other arithmetic, per_device(): return result.reshape(rows, depth, cells) + constant[None]  2.92 us

profile of v5, /device:TPU:0, one launch (start us, length us, event | category | flops | bytes accessed | tf_op | source)
XLA Modules:
  0.0 62.1 jit_solution(15384253955017316867)
XLA Ops:
  0.0 59.2 %bgk_steps.1 = (f32[2048,128]{1,0:T(8,128)}, f32[1,256]{1,0:T(1,128)}) custom-call(s32[8,12]{1,0:T(8,128)} %cols_ref.1, bf16[8,128,1536]{2,1,0:T(8,128)(2,1)} %tiles_ref.1, f32[2048,128]{1,0:T(8,128)} %bitcast.4, f32[1,256]{1,0:T(1,128)} %relax_ref.1, f32[1,1024]{1,0:T(1,128)} %bitcast.6), custom_call_target="tpu_custom_call" | custom-call | tf_op jit(solution)/shard_map/bgk_steps/pallas_call | solution.py:451
  59.2 2.9 %broadcast_add_fusion = f32[1024,1,256]{2,1,0:T(1,128)} fusion(f32[1024,1,256]{2,1,0:T(1,128)} %bitcast.5, f32[256]{0:T(256)} %bitcast.7), kind=kLoop, calls=%fused_computation | loop fusion | flops 262144 | bytes 2098176 | tf_op jit(solution)/shard_map/add | solution.py:498

commit v6 on v3

--- a/solution.py
+++ b/solution.py
@@ -66,7 +66,7 @@
 
 
 def kernel(
-    count, slabs, cols_ref, tiles_ref, dist_ref, relax_ref, weight_ref, out_ref, constant_ref,
+    count, slabs, place_ref, tiles_ref, dist_ref, relax_ref, weight_ref, out_ref, constant_ref,
     tiles, dense, source_rows, relax, node_weight, state, acc, gathered, plane_out, plane_in,
     mom_out, mom_in, gram_out, gram_in, weights2, tile_sem, source_sem, small_sem, vert_send,
     vert_recv, plane_send, plane_recv, mom_send, mom_recv, gram_send, gram_recv,
@@ -205,17 +205,15 @@
         load.wait()
     per_chunk = CHUNK // TILE
 
-    def expand(r, carry):
-        columns = [cols_ref[r, j] for j in range(listed)]
+    def expand(index, carry):
+        k, r = lax.div(index, row_blocks), lax.rem(index, row_blocks)
         here = pl.ds(pl.multiple_of(r * TILE, TILE), TILE)
-        for c in range(RBLK):
-            place = listed
-            for j in range(listed):
-                place = jnp.where(columns[j] == c, j, place)
-            dense[c // per_chunk, here, pl.ds(c % per_chunk * TILE, TILE)] = tiles[place, r]
+        for b in range(per_chunk):
+            place = place_ref[r, k * per_chunk + b]
+            dense[k, here, pl.ds(b * TILE, TILE)] = tiles[place, r]
         return carry
 
-    lax.fori_loop(0, row_blocks, expand, 0)
+    lax.fori_loop(0, (V // CHUNK) * row_blocks, expand, 0, unroll=4)
 
     def advect(step):
         for half in range(HALVES):
@@ -251,12 +249,17 @@
             flux += jnp.maximum(pz, 0.0) * (source - lower_z) + jnp.minimum(pz, 0.0) * (
                 upper_z - source
             )
-            acc[pl.ds(base, PART), :] = source - flux
+            result = source - flux
+            if step == 0:
+                acc[pl.ds(base, PART), :] = result
+            else:
+                acc[pl.ds(base, PART), pl.ds(0, lanes)] += result[:, :lanes]
+                acc[pl.ds(base, PART), pl.ds(lanes, cells - lanes)] = result[:, lanes:]
             return carry
 
         lax.fori_loop(0, rows // PART, one, 0)
 
-    def multiply(stage, indices):
+    def multiply(stage, indices, fresh=False):
         side = pl.ds(stage % HALVES * lanes, lanes)
 
         def one(i, carry):
@@ -266,7 +269,10 @@
                 total += jnp.dot(
                     dense[index, here, :], gathered[stage, index], preferred_element_type=F32
                 )
-            acc[here, side] += KERNEL_STEP * total
+            if fresh:
+                acc[here, side] = KERNEL_STEP * total
+            else:
+                acc[here, side] += KERNEL_STEP * total
             return carry
 
         lax.fori_loop(0, rows // CHUNK, one, 0, unroll=True)
@@ -281,13 +287,15 @@
         for item in early:
             arrive(stage, item)
 
-    def collide(stage):
+    def kernel_term(stage, fresh=False):
         ready = [me * chunks + chunk for chunk in range(chunks)]
-        multiply(stage, ready + [block * chunks + chunk for _, block, chunk in early])
+        multiply(stage, ready + [block * chunks + chunk for _, block, chunk in early], fresh)
         for at in range(0, len(rest), 2):
             for item in rest[at : at + 2]:
                 arrive(stage, item)
             multiply(stage, [block * chunks + chunk for _, block, chunk in rest[at : at + 2]])
+
+    def send_moments(stage):
         side = pl.ds(stage % HALVES * lanes, lanes)
         total = jnp.zeros((16, lanes), F32)
         for base in range(0, rows, CHUNK):
@@ -356,18 +364,22 @@
     relay(0)
     send_own(1, own[len(own) // 2 :])
     advect(0)
-    collide(0)
+    kernel_term(0)
+    send_moments(0)
     relay(1)
     inverse = invert()
     relax_half(0, inverse)
-    collide(1)
+    kernel_term(1)
+    send_moments(1)
     relay(2)
     relax_half(1, inverse)
+    kernel_term(2, fresh=True)
+    relay(3)
     advect(1)
-    collide(2)
-    relay(3)
+    send_moments(2)
+    kernel_term(3)
+    send_moments(3)
     relax_half(2, inverse)
-    collide(3)
     relax_half(3, inverse)
 
     for copy in pending:
@@ -379,6 +391,9 @@
     assert depth == 1 and cells == 256 and rows % CHUNK == 0
     row_blocks, listed = tile_cols.shape
     chunks = rows // CHUNK
+    slots = jnp.arange(listed, dtype=jnp.int32)[None, :, None]
+    match = tile_cols[:, :, None] == jnp.arange(RBLK, dtype=jnp.int32)[None, None, :]
+    places = listed + jnp.sum(jnp.where(match, slots - listed, 0), axis=1)
     keys = 3 * chunks if count == 4 else (count - 1) * chunks
     peers = count - 1
     stages = STEPS * HALVES
@@ -426,7 +441,7 @@
         ),
         name="bgk_steps",
     )(
-        tile_cols, kernel_tiles, distribution.reshape(rows * HALVES, lanes), relax_rate,
+        places, kernel_tiles, distribution.reshape(rows * HALVES, lanes), relax_rate,
         node_weight.reshape(1, rows),
     )
     return result.reshape(rows, depth, cells) + constant[None]

time: 56.6 us -> 55.7 us (0.984)
  Pallas kernels: 53.5 us -> 51.1 us
  local copies, waits for them, and re-layouts: 0 us -> 0.77 us
  other arithmetic: 2.92 us -> 3.61 us
    pallas_call x1, Pallas kernels: 53.5 us -> 51.1 us  [per_device(): pl.pallas_call(functools.partial(kernel, count, slabs), out_shape=(jax.Sh...]
    unnamed x0 -> x1, local copies, waits for them, and re-layouts: none -> 0.77 us
    add x0 -> x1, other arithmetic: none -> 0.6 us  [per_device(): places = listed + jnp.sum(jnp.where(match, slots - listed, 0), axis=1)]
where the time goes in v6:
time: 55.7 us; the launch traced here: 55.5 us
  Pallas kernels  51.1 us (92%)
  other arithmetic  3.61 us (6%)
  local copies, waits for them, and re-layouts  0.77 us (1%)
    pallas_call x1, Pallas kernels, per_device(): pl.pallas_call(functools.partial(kernel, count, slabs), out_shape=(jax.Sh...  51.1 us
    add x1, other arithmetic, per_device(): return result.reshape(rows, depth, cells) + constant[None]  2.92 us

profile of v6, /device:TPU:0, one launch (start us, length us, event | category | flops | bytes accessed | tf_op | source)
XLA Modules:
  0.0 55.5 jit_solution(5298966333144122048)
XLA Ops:
  0.0 0.8 %copy.7 = s32[8,12]{0,1:T(8,128)S(1)} copy(s32[8,12]{1,0:T(8,128)} %param.9) | data formatting | bytes 768 | tf_op args[4]
  0.8 0.1 select_reduce_fusion
  0.9 0.6 %broadcast_add_fusion.1.place_ref = s32[8,32]{1,0:T(8,128)} fusion(s32[8,32]{1,0:T(8,128)S(1)} %select_reduce_fusion), kind=kLoop, calls=%fused_computation.3 | loop fusion | flops 256 | bytes 2048 | tf_op jit(solution)/shard_map/add | solution.py:396
  1.5 51.1 %bgk_steps.1 = (f32[2048,128]{1,0:T(8,128)}, f32[1,256]{1,0:T(1,128)}) custom-call(s32[8,32]{1,0:T(8,128)} %broadcast_add_fusion.1.place_ref, bf16[8,128,1536]{2,1,0:T(8,128)(2,1)} %tiles_ref.1, f32[2048,128]{1,0:T(8,128)} %bitcast.4, f32[1,256]{1,0:T(1,128)} %relax_ref.1, f32[1,1024]{1,0:T(1,128)} %bitcast.6), custom_call_target="tpu_custom_call" | custom-call | tf_op jit(solution)/shard_map/bgk_steps/pallas_call | solution.py:403
  52.6 2.9 %broadcast_add_fusion = f32[1024,1,256]{2,1,0:T(1,128)} fusion(f32[1024,1,256]{2,1,0:T(1,128)} %bitcast.5, f32[256]{0:T(256)} %bitcast.7), kind=kLoop, calls=%fused_computation | loop fusion | flops 262144 | bytes 2098176 | tf_op jit(solution)/shard_map/add | solution.py:447
  (1 shorter events, 0.0 us)

commit v7 on v6

--- a/solution.py
+++ b/solution.py
@@ -364,10 +364,10 @@
     relay(0)
     send_own(1, own[len(own) // 2 :])
     advect(0)
+    inverse = invert()
     kernel_term(0)
     send_moments(0)
     relay(1)
-    inverse = invert()
     relax_half(0, inverse)
     kernel_term(1)
     send_moments(1)

time: 55.7 us -> 55.9 us (level)
  no operation moved by 1% of the time
where the time goes in v7:
time: 55.9 us; the launch traced here: 55.7 us
  Pallas kernels  51.3 us (92%)
  other arithmetic  3.61 us (6%)
  local copies, waits for them, and re-layouts  0.77 us (1%)
    pallas_call x1, Pallas kernels, per_device(): pl.pallas_call(functools.partial(kernel, count, slabs), out_shape=(jax.Sh...  51.3 us
    add x1, other arithmetic, per_device(): return result.reshape(rows, depth, cells) + constant[None]  2.92 us

profile of v7, /device:TPU:0, one launch (start us, length us, event | category | flops | bytes accessed | tf_op | source)
XLA Modules:
  0.0 55.7 jit_solution(7059897447871676701)
XLA Ops:
  0.0 0.8 %copy.7 = s32[8,12]{0,1:T(8,128)S(1)} copy(s32[8,12]{1,0:T(8,128)} %param.9) | data formatting | bytes 768 | tf_op args[4]
  0.8 0.1 select_reduce_fusion
  0.9 0.6 %broadcast_add_fusion.1.place_ref = s32[8,32]{1,0:T(8,128)} fusion(s32[8,32]{1,0:T(8,128)S(1)} %select_reduce_fusion), kind=kLoop, calls=%fused_computation.3 | loop fusion | flops 256 | bytes 2048 | tf_op jit(solution)/shard_map/add | solution.py:396
  1.5 51.3 %bgk_steps.1 = (f32[2048,128]{1,0:T(8,128)}, f32[1,256]{1,0:T(1,128)}) custom-call(s32[8,32]{1,0:T(8,128)} %broadcast_add_fusion.1.place_ref, bf16[8,128,1536]{2,1,0:T(8,128)(2,1)} %tiles_ref.1, f32[2048,128]{1,0:T(8,128)} %bitcast.4, f32[1,256]{1,0:T(1,128)} %relax_ref.1, f32[1,1024]{1,0:T(1,128)} %bitcast.6), custom_call_target="tpu_custom_call" | custom-call | tf_op jit(solution)/shard_map/bgk_steps/pallas_call | solution.py:403
  52.8 2.9 %broadcast_add_fusion = f32[1024,1,256]{2,1,0:T(1,128)} fusion(f32[1024,1,256]{2,1,0:T(1,128)} %bitcast.5, f32[256]{0:T(256)} %bitcast.7), kind=kLoop, calls=%fused_computation | loop fusion | flops 262144 | bytes 2098176 | tf_op jit(solution)/shard_map/add | solution.py:447
  (1 shorter events, 0.0 us)
